TPU v7x, 32 devices: a whole 2x2x4 slice. The times are simulated.
32 devices in a mesh: rep: 4 (over z), ctx: 4 (over y, core), shard: 2 (over x).
Axes of the slice: x: 2, y: 2, z: 4, core: 2. Of those that a mesh axis runs over, the one named last changes fastest.
Arguments:
- tokens: bfloat16 [4, 512, 2, 2048], P('rep', 'ctx', 'shard'), may hold values from -6 to 6
- cotangent: bfloat16 [4, 512, 2, 2048], P('rep', 'ctx', 'shard'), may hold values from -6 to 6
- span_order: int32 [4, 2, 8], P('rep', 'shard'), may hold values from 0 to 7, each once within a row
- w_qkv: float32 [2048, 6144], P(('ctx', 'shard')), may hold values from -0.125 to 0.125
- w_out: float32 [2048, 2048], P(('ctx', 'shard')), may hold values from -0.75 to 0.75
- w_up: float32 [2048, 11264], P(('ctx', 'shard')), may hold values from -0.125 to 0.125
- w_down: float32 [5632, 2048], P(('ctx', 'shard')), may hold values from -0.078125 to 0.078125
- norm_params: float32 [7, 2048], replicated, may hold values from -2 to 2, as said below
- m_qkv: float32 [2048, 6144], P(('ctx', 'shard')), may hold values from -64 to 64
- v_qkv: float32 [2048, 6144], P(('ctx', 'shard')), may hold values from 4.096 to 65.536
- m_out: float32 [2048, 2048], P(('ctx', 'shard')), may hold values from -6 to 6
- v_out: float32 [2048, 2048], P(('ctx', 'shard')), may hold values from 0.08192 to 1.2288
- m_up: float32 [2048, 11264], P(('ctx', 'shard')), may hold values from -16 to 16
- v_up: float32 [2048, 11264], P(('ctx', 'shard')), may hold values from 0.32768 to 5.3248
- m_down: float32 [5632, 2048], P(('ctx', 'shard')), may hold values from -24 to 24
- v_down: float32 [5632, 2048], P(('ctx', 'shard')), may hold values from 0.73728 to 12.288
- m_norm: float32 [7, 2048], replicated, may hold values from -80 to 80
- v_norm: float32 [7, 2048], replicated, may hold values from 4.096 to 65.536
Outputs:
- block_output: bfloat16 [4, 512, 2, 2048], P('rep', 'ctx', 'shard')
- input_grad: float32 [4, 512, 2, 2048], P('rep', 'ctx', 'shard')
- new_m_qkv: float32 [2048, 6144], P(('ctx', 'shard'))
- new_v_qkv: float32 [2048, 6144], P(('ctx', 'shard'))
- new_w_qkv: float32 [2048, 6144], P(('ctx', 'shard'))
- new_m_out: float32 [2048, 2048], P(('ctx', 'shard'))
- new_v_out: float32 [2048, 2048], P(('ctx', 'shard'))
- new_w_out: float32 [2048, 2048], P(('ctx', 'shard'))
- new_m_up: float32 [2048, 11264], P(('ctx', 'shard'))
- new_v_up: float32 [2048, 11264], P(('ctx', 'shard'))
- new_w_up: float32 [2048, 11264], P(('ctx', 'shard'))
- new_m_down: float32 [5632, 2048], P(('ctx', 'shard'))
- new_v_down: float32 [5632, 2048], P(('ctx', 'shard'))
- new_w_down: float32 [5632, 2048], P(('ctx', 'shard'))
- new_m_norm: float32 [7, 2048], replicated
- new_v_norm: float32 [7, 2048], replicated
- new_norm_params: float32 [7, 2048], replicated
Inputs may be any that keep to these rules, and one draw needn't show every extreme that they name: `span_order`: each row is a permutation of 0 to 7. `norm_params`: rows 0 and 2 lie between 0.4 and 1.6.
All inputs are finite; a program needn't handle non-finite values.
Results may differ from a plain program's by a relative error of at most 0.018.
Values may be sent and summed in bfloat16 or wider, within the bound.
No kernel may reach another device: no remote copies, remote signals or barrier semaphores. Data moves between devices by JAX's collectives and lax.ppermute only.
A program may use at most 832 MiB of HBM per device.

v0:
```python
import functools

import jax
import jax.numpy as jnp
from jax import lax
from jax.experimental import pallas as pl
from jax.experimental.pallas import tpu as pltpu
from jax.sharding import PartitionSpec as P

HEADS = 32
HEAD_DIM = 64
FF = 5632
ROTARY = 16
STEP = 10

eps_norm = 1e-05
masked_score = -1e30
beta_one = 0.9
beta_two = 0.999
adam_eps = 1e-08
weight_decay = 0.1
score_scale = HEAD_DIM ** (-0.5)
FIRST = (((0,), (0,)), ((), ()))
LAST = (((1,), (1,)), ((), ()))
PLAIN = (((1,), (0,)), ((), ()))
bf16 = jnp.bfloat16
f32 = jnp.float32


def dot(a, b, dims):
    return lax.dot_general(a, b, dims, preferred_element_type=f32)


def adam_update(weight, moment_one, moment_two, grad, step_rate, decay_rate):
    first_new = beta_one * moment_one + (1.0 - beta_one) * grad
    second_new = beta_two * moment_two + (1.0 - beta_two) * grad * grad
    first_hat = first_new / (1.0 - beta_one**STEP)
    second_hat = second_new / (1.0 - beta_two**STEP)
    weight_new = weight - step_rate * (
        first_hat / (jnp.sqrt(second_hat) + adam_eps) + decay_rate * weight
    )
    return (first_new, second_new, weight_new)


class Plane:
    def __init__(self):
        self.s_size = lax.axis_size("shard")
        self.ctx_size = lax.axis_size("ctx")
        self.y_size = self.ctx_size // 2
        self.ctx = lax.axis_index("ctx")
        self.s = lax.axis_index("shard")
        self.y = self.ctx // 2
        self.c = self.ctx % 2
        self.blocks = self.ctx_size * self.s_size

    def core(self, x):
        return lax.ppermute(x, "ctx", [(i, i ^ 1) for i in range(self.ctx_size)])

    def along(self, x, axis, step):
        if axis == "y":
            return lax.ppermute(x, "ctx", [(i, i ^ (2 * step)) for i in range(self.ctx_size)])
        return lax.ppermute(x, "shard", [(i, i ^ step) for i in range(self.s_size)])

    def index(self, axis):
        return self.y if axis == "y" else self.s

    def steps(self, flip):
        ys = []
        k = self.y_size // 2
        while k:
            ys.append(("y", k))
            k //= 2
        ss = []
        k = self.s_size // 2
        while k:
            ss.append(("s", k))
            k //= 2
        return ys + ss if flip else ss + ys

    def chip_exchange(self, x, take):
        out = [(self.y, self.s, take(self.y, self.s))]
        for ry in range(self.y_size):
            for rs in range(self.s_size):
                if ry or rs:
                    y, s = self.y ^ ry, self.s ^ rs
                    mask = 2 * ry * self.s_size + rs
                    perm = [(i, i ^ mask) for i in range(self.blocks)]
                    out.append((y, s, lax.ppermute(take(y, s), ("ctx", "shard"), perm)))
        return out

    def sum_all(self, x):
        for axis, step in self.steps(False):
            x = x + self.along(x, axis, step)
        return x + self.core(x)

    def scatter_sum(self, p, flip):
        axes = {"y": 1, "s": 2}
        steps = self.steps(flip)
        kept = got = None
        for n, (axis, step) in enumerate(steps):
            ax = axes[axis]
            bit = (self.index(axis) // step) % 2
            kept = lax.dynamic_slice_in_dim(p, bit * step, step, ax)
            send = lax.dynamic_slice_in_dim(p, (1 - bit) * step, step, ax)
            got = self.along(send, axis, step)
            if n + 1 < len(steps):
                p = (kept.astype(f32) + got.astype(f32)).astype(bf16)
        return kept[:, 0, 0], got[:, 0, 0]

    def gather(self, p, flip):
        axes = {"y": 1, "s": 2}
        p = p[:, None, None]
        for axis, step in reversed(self.steps(flip)):
            ax = axes[axis]
            bit = (self.index(axis) // step) % 2
            got = self.along(p, axis, step)
            first = bit == 0
            p = jnp.concatenate([jnp.where(first, p, got), jnp.where(first, got, p)], ax)
        return p


class Order:
    def __init__(self):
        self.last = None

    def __call__(self, stage, *args):
        if self.last is not None:
            args, self.last = lax.optimization_barrier((args, self.last))
        out = stage(*args)
        self.last = jax.tree.leaves(out)[0]
        return out


SMALL = pl.CostEstimate(flops=1024, bytes_accessed=1024, transcendentals=0)


class RepSum:
    def __init__(self, order):
        self.order = order
        z = lax.axis_index("rep")
        self.end = (z == 0) | (z == lax.axis_size("rep") - 1)
        self.queue = []
        self.flight = []
        self.depth = 1
        self.done = {}

    def push(self, name, g):
        self.queue.append((name, g))

    def busy(self):
        return bool(self.queue or self.flight)

    def tick(self, between=None):
        old = {}
        if len(self.flight) >= self.depth or (self.flight and not self.queue):
            old = self.flight.pop(0)
        new = self.queue.pop(0) if self.queue else None
        values = {}
        if "in" in old:
            values["g"], values["g_got"] = old["in"][1], old["in_got"]
        if "mid" in old:
            values["s"], values["s_got"] = old["mid"][1], old["mid_got"]
        if new:
            values["new"] = new[1]
        both = new and "mid" in old and new[1].shape == old["mid"][1].shape
        if "out" in old:
            values["out_got"] = old["out_got"]

        def stage(v):
            def add(a, b):
                return lax.reduce_precision(a.astype(f32) + b.astype(f32), 8, 7).astype(bf16)

            out = {}
            if "g" in v:
                out["a_sum"] = add(v["g"], v["g_got"])
            if "s" in v:
                total = add(v["s"], v["s_got"])
                out["total"] = jnp.where(self.end, v["new"], total) if both else total
            if "new" in v and not both:
                out["new"] = v["new"]
            if "out_got" in v:
                out["z_got"] = v["out_got"]
            return out

        if not values:
            return
        out = self.order(stage, values)
        if between is not None:
            out, self.kept = lax.optimization_barrier((out, between()))
        if "out" in old:
            self.done[old["out"][0]] = jnp.where(self.end, out["z_got"], old["out"][1])
        slot = {}
        if both:
            got = lax.ppermute(out["total"], "rep", [(0, 1), (1, 0), (2, 3), (3, 2)])
            slot = {"in": new, "in_got": got, "out": (old["mid"][0], out["total"]), "out_got": got}
        else:
            if new:
                slot["in"] = new
                slot["in_got"] = lax.ppermute(out["new"], "rep", [(0, 1), (3, 2)])
            if "mid" in old:
                slot["out"] = (old["mid"][0], out["total"])
                slot["out_got"] = lax.ppermute(out["total"], "rep", [(1, 0), (2, 3)])
        if "in" in old:
            slot["mid"] = (old["in"][0], out["a_sum"])
            slot["mid_got"] = lax.ppermute(out["a_sum"], "rep", [(1, 2), (2, 1)])
        if slot:
            self.flight.append(slot)


def cast_kernel(w_ref, out_ref):
    out_ref[...] = w_ref[...].astype(bf16)


def cast(w):
    rows, width = w.shape
    unit = max(n for n in (128, 256, 512, 1024, 1408, 2048, 2816) if width % n == 0)
    spec = pl.BlockSpec((rows, unit), lambda i: (0, i))
    return pl.pallas_call(
        cast_kernel,
        grid=(width // unit,),
        in_specs=[spec],
        out_specs=spec,
        out_shape=jax.ShapeDtypeStruct(w.shape, bf16),
        compiler_params=pltpu.CompilerParams(vmem_limit_bytes=48 * 1024 * 1024),
        cost_estimate=SMALL,
    )(w)


def gated_kernel(ga_ref, gb_ref, ua_ref, ub_ref, grad_ref, gains_ref, g0_ref, g1_ref, u0_ref, u1_ref, act_ref, sums_ref):
    half = g0_ref.shape[1]
    gate = ga_ref[...].astype(f32) + gb_ref[...].astype(f32)
    up = ua_ref[...].astype(f32) + ub_ref[...].astype(f32)
    sig = jax.nn.sigmoid(gate)
    silu = gate * sig
    grad = grad_ref[...]
    act_ref[...] = (silu * up).astype(bf16)
    ggate = (grad * up * sig * (1.0 + gate * (1.0 - sig))).astype(bf16)
    gup = (grad * silu).astype(bf16)
    g0_ref[...] = ggate[:, :half]
    g1_ref[...] = ggate[:, half:]
    u0_ref[...] = gup[:, :half]
    u1_ref[...] = gup[:, half:]
    a, b = ggate.astype(f32), gup.astype(f32)
    e = jnp.sum(a * gains_ref[:, 0:1] + b * gains_ref[:, 2:3], axis=0, keepdims=True)
    ez = jnp.sum(a * (gate - gains_ref[:, 1:2]) + b * (up - gains_ref[:, 3:4]), axis=0, keepdims=True)
    both = jnp.concatenate([e, ez], axis=0)

    @pl.when(pl.program_id(0) == 0)
    def _():
        sums_ref[...] = both

    @pl.when(pl.program_id(0) > 0)
    def _():
        sums_ref[...] += both


def gated(ga, gb, ua, ub, grad_act, gains):
    rows, t = grad_act.shape
    n = max(n for n in (1, 2, 4) if rows % (16 * n) == 0)
    whole = pl.BlockSpec((rows // n, t), lambda i: (i, 0))
    half = pl.BlockSpec((rows // n, t // 2), lambda i: (i, 0))
    out_half = jax.ShapeDtypeStruct((rows, t // 2), bf16)
    return pl.pallas_call(
        gated_kernel,
        grid=(n,),
        in_specs=[whole] * 5 + [pl.BlockSpec((rows // n, 4), lambda i: (i, 0))],
        out_specs=[half] * 4 + [whole, pl.BlockSpec((2, t), lambda i: (0, 0))],
        out_shape=[out_half] * 4 + [jax.ShapeDtypeStruct((rows, t), bf16), jax.ShapeDtypeStruct((2, t), f32)],
        compiler_params=pltpu.CompilerParams(vmem_limit_bytes=56 * 1024 * 1024),
        cost_estimate=SMALL,
    )(ga, gb, ua, ub, grad_act, gains)


def own_columns_kernel(block_ref, x_ref, out_ref):
    out_ref[...] = x_ref[...].T


def own_columns(x, block, width):
    rows = x.shape[0]
    if width % 128:
        return lax.dynamic_slice_in_dim(x, block[0] * width, width, 1).T
    tile = min(rows, 512)
    return pl.pallas_call(
        own_columns_kernel,
        grid_spec=pltpu.PrefetchScalarGridSpec(
            num_scalar_prefetch=1,
            grid=(rows // tile,),
            in_specs=[pl.BlockSpec((tile, width), lambda i, block: (i, block[0]))],
            out_specs=pl.BlockSpec((width, tile), lambda i, block: (0, i)),
        ),
        out_shape=jax.ShapeDtypeStruct((width, rows), bf16),
        compiler_params=pltpu.CompilerParams(vmem_limit_bytes=48 * 1024 * 1024),
        cost_estimate=SMALL,
    )(block, x)


def split_kernel(core_ref, w_ref, mine_ref, theirs_ref):
    unit = mine_ref.shape[0]
    first = core_ref[0] == 0
    a, b = w_ref[:, :unit], w_ref[:, unit:]
    mine_ref[...] = jnp.where(first, a, b).T.astype(bf16)
    theirs_ref[...] = jnp.where(first, b, a).T.astype(bf16)


def split_columns(w, core, lead, unit, count):
    rows = w.shape[0]
    half = pl.BlockSpec((unit, rows), lambda j, core: (j, 0))
    out = jax.ShapeDtypeStruct((count * unit, rows), bf16)
    return pl.pallas_call(
        split_kernel,
        grid_spec=pltpu.PrefetchScalarGridSpec(
            num_scalar_prefetch=1,
            grid=(count,),
            in_specs=[pl.BlockSpec((rows, 2 * unit), lambda j, core: (0, lead + j))],
            out_specs=[half, half],
        ),
        out_shape=[out, out],
        compiler_params=pltpu.CompilerParams(vmem_limit_bytes=32 * 1024 * 1024),
        cost_estimate=SMALL,
    )(core, w)


def arrange_kernel(at_ref, a_ref, b_ref, c_ref, d_ref, send_ref, keep_ref):
    send_ref[...] = jnp.concatenate([a_ref[...], b_ref[...]], axis=1)
    keep_ref[...] = jnp.concatenate([c_ref[...], d_ref[...]], axis=1)


def arrange(mine, got, place, pre, y_size, s_size, unit, flip):
    r = mine.shape[1]
    half = pre * y_size * s_size // 2

    def block(i, place, keep):
        p = i % pre
        i = i // pre
        if flip:
            s, y = i % s_size, i // s_size
            bit = place[0] // (y_size // 2)
            bit = bit if keep else 1 - bit
            y = y + bit * (y_size // 2)
        else:
            y, s = i % y_size, i // y_size
            bit = place[1] // (s_size // 2)
            bit = bit if keep else 1 - bit
            s = s + bit * (s_size // 2)
        return ((p * y_size + y) * s_size + s, 0)

    def spec(keep):
        return pl.BlockSpec((unit, r), lambda i, place: block(i, place, keep))

    out = jax.ShapeDtypeStruct((half * unit, 2 * r), bf16)
    out_spec = pl.BlockSpec((unit, 2 * r), lambda i, place: (i, 0))
    return pl.pallas_call(
        arrange_kernel,
        grid_spec=pltpu.PrefetchScalarGridSpec(
            num_scalar_prefetch=1,
            grid=(half,),
            in_specs=[spec(False), spec(False), spec(True), spec(True)],
            out_specs=[out_spec, out_spec],
        ),
        out_shape=[out, out],
        compiler_params=pltpu.CompilerParams(vmem_limit_bytes=32 * 1024 * 1024),
        cost_estimate=SMALL,
    )(place, mine, got, mine, got)


def product_kernel(dims, a_ref, b_ref, *refs):
    p = dot(a_ref[...], b_ref[...], dims)
    if len(refs) == 2:
        p = p + refs[0][...]
    refs[-1][...] = p.astype(refs[-1].dtype)


def mm(a, b, dims, dtype, tm=None, tn=None, add=None):
    (ca,), (cb,) = dims[0]
    m, k, n = a.shape[1 - ca], a.shape[ca], b.shape[1 - cb]
    tm, tn = tm or m, tn or n
    a_block = [0, 0]
    a_block[ca], a_block[1 - ca] = k, tm
    b_block = [0, 0]
    b_block[cb], b_block[1 - cb] = k, tn
    out = pl.BlockSpec((tm, tn), lambda i, j: (i, j))
    return pl.pallas_call(
        functools.partial(product_kernel, dims),
        grid=(m // tm, n // tn),
        in_specs=[
            pl.BlockSpec(tuple(a_block), (lambda i, j: (0, i)) if ca == 0 else (lambda i, j: (i, 0))),
            pl.BlockSpec(tuple(b_block), (lambda i, j: (0, j)) if cb == 0 else (lambda i, j: (j, 0))),
        ]
        + ([] if add is None else [out]),
        out_specs=out,
        out_shape=jax.ShapeDtypeStruct((m, n), dtype),
        compiler_params=pltpu.CompilerParams(vmem_limit_bytes=48 * 1024 * 1024),
        cost_estimate=SMALL,
    )(*((a, b) if add is None else (a, b, add)))


def last_step_kernel(bits_ref, own0_ref, got0_ref, own1_ref, got1_ref, out_ref):
    y, s = pl.program_id(1), pl.program_id(2)
    half = own0_ref.shape[3]
    ys, ss = bits_ref[2], bits_ref[3]
    a = jnp.where(s // ss == bits_ref[1], own0_ref[0, 0], got0_ref[0, 0])
    b = jnp.where(y // ys == bits_ref[0], own1_ref[0, 0], got1_ref[0, 0])
    out_ref[0, 0, 0, :, :half] = a
    out_ref[0, 0, 0, :, half:] = b


def last_step(parts, got, bits, pre, y_size, s_size):
    rows, half = parts[0].shape[2] // pre, parts[0].shape[3]
    along_s = pl.BlockSpec((1, 1, rows, half), lambda p, y, s, bits: (y, s % (s_size // 2), p, 0))
    along_y = pl.BlockSpec((1, 1, rows, half), lambda p, y, s, bits: (y % (y_size // 2), s, p, 0))
    return pl.pallas_call(
        last_step_kernel,
        grid_spec=pltpu.PrefetchScalarGridSpec(
            num_scalar_prefetch=1,
            grid=(pre, y_size, s_size),
            in_specs=[along_s, along_s, along_y, along_y],
            out_specs=pl.BlockSpec((1, 1, 1, rows, 2 * half), lambda p, y, s, bits: (p, y, s, 0, 0)),
        ),
        out_shape=jax.ShapeDtypeStruct((pre, y_size, s_size, rows, 2 * half), bf16),
        compiler_params=pltpu.CompilerParams(vmem_limit_bytes=48 * 1024 * 1024),
        cost_estimate=SMALL,
    )(bits, parts[0], got[0], parts[1], got[1])


def stack_turned_kernel(a_ref, b_ref, out_ref):
    r = a_ref.shape[1]
    out_ref[:r] = a_ref[...].T
    out_ref[r:] = b_ref[...].T


def stack_turned(a, b):
    rows, width = a.shape
    n = max(n for n in (1, 2, 4, 6, 8, 11) if rows % (128 * n) == 0)
    spec = pl.BlockSpec((rows // n, width), lambda i: (i, 0))
    return pl.pallas_call(
        stack_turned_kernel,
        grid=(n,),
        in_specs=[spec, spec],
        out_specs=pl.BlockSpec((2 * width, rows // n), lambda i: (0, i)),
        out_shape=jax.ShapeDtypeStruct((2 * width, rows), bf16),
        compiler_params=pltpu.CompilerParams(vmem_limit_bytes=48 * 1024 * 1024),
        cost_estimate=SMALL,
    )(a, b)


def add_split_kernel(bit_ref, a_ref, b_ref, c_ref, d_ref, send_ref, keep_ref):
    send_ref[...] = (a_ref[...].astype(f32) + b_ref[...].astype(f32)).astype(bf16)
    keep_ref[...] = (c_ref[...].astype(f32) + d_ref[...].astype(f32)).astype(bf16)


def add_split(kept, got, bit):
    rows, t = kept.shape
    half = rows // 2
    n = max(n for n in (1, 2, 3, 4) if half % (16 * n) == 0)
    rb = half // n
    away = pl.BlockSpec((rb, t), lambda i, bit: ((1 - bit[0]) * n + i, 0))
    here = pl.BlockSpec((rb, t), lambda i, bit: (bit[0] * n + i, 0))
    out = jax.ShapeDtypeStruct((half, t), bf16)
    out_spec = pl.BlockSpec((rb, t), lambda i, bit: (i, 0))
    return pl.pallas_call(
        add_split_kernel,
        grid_spec=pltpu.PrefetchScalarGridSpec(
            num_scalar_prefetch=1,
            grid=(n,),
            in_specs=[away, away, here, here],
            out_specs=[out_spec, out_spec],
        ),
        out_shape=[out, out],
        compiler_params=pltpu.CompilerParams(vmem_limit_bytes=48 * 1024 * 1024),
        cost_estimate=SMALL,
    )(bit, kept, got, kept, got)


def token_rows_kernel(core_ref, a_ref, b_ref, c_ref, d_ref, out_ref):
    mine = core_ref[0] == pl.program_id(2)
    half = out_ref.shape[0] // 2
    out_ref[:half] = jnp.where(mine, a_ref[0, 0], c_ref[0, 0])
    out_ref[half:] = jnp.where(mine, b_ref[0, 0], d_ref[0, 0])


def token_rows(mine, theirs, core):
    y_size, s_size, rows, width = mine[0].shape
    part = pl.BlockSpec((1, 1, rows, width), lambda s, y, c, core: (y, s, 0, 0))
    return pl.pallas_call(
        token_rows_kernel,
        grid_spec=pltpu.PrefetchScalarGridSpec(
            num_scalar_prefetch=1,
            grid=(s_size, y_size, 2),
            in_specs=[part] * 4,
            out_specs=pl.BlockSpec((2 * rows, width), lambda s, y, c, core: ((s * y_size + y) * 2 + c, 0)),
        ),
        out_shape=jax.ShapeDtypeStruct((s_size * y_size * 4 * rows, width), bf16),
        compiler_params=pltpu.CompilerParams(vmem_limit_bytes=32 * 1024 * 1024),
        cost_estimate=SMALL,
    )(core, *mine, *theirs)


def adam_kernel(rate, two, core_ref, w_ref, m_ref, v_ref, *refs):
    grad = refs[0][...].astype(f32)
    if two:
        other = refs[1][...].astype(f32)
        mine = core_ref[0] == 0
        grad = jnp.concatenate([jnp.where(mine, grad, other), jnp.where(mine, other, grad)], axis=1)
    new_m_ref, new_v_ref, new_w_ref = refs[-3:]
    new_m, new_v, new_w = adam_update(w_ref[...], m_ref[...], v_ref[...], grad, rate, weight_decay)
    new_m_ref[...] = new_m
    new_v_ref[...] = new_v
    new_w_ref[...] = new_w


def adam_part(state, grads, core, rate, prev, row_first, lead, unit, rb):
    w, m, v = state
    two = len(grads) == 2
    rows, width = grads[0].shape
    whole = pl.BlockSpec((rb, unit * len(grads)), lambda i, g, core: (row_first // rb + i, lead + g))
    half = pl.BlockSpec((rb, unit), lambda i, g, core: (i, g))
    out = jax.ShapeDtypeStruct(w.shape, f32)
    extra, aliases = [], {}
    if prev is not None:
        extra = list(prev)
        aliases = {4 + len(grads) + i: i for i in range(3)}
    return pl.pallas_call(
        functools.partial(adam_kernel, rate, two),
        grid_spec=pltpu.PrefetchScalarGridSpec(
            num_scalar_prefetch=1,
            grid=(rows // rb, width // unit),
            in_specs=[whole] * 3 + [half] * len(grads) + [pl.BlockSpec(memory_space=pl.ANY)] * len(extra),
            out_specs=[whole] * 3,
        ),
        out_shape=[out] * 3,
        input_output_aliases=aliases,
        compiler_params=pltpu.CompilerParams(vmem_limit_bytes=48 * 1024 * 1024),
        cost_estimate=SMALL,
    )(core, w, m, v, *grads, *extra)


def attend_kernel(kept_ref, got_ref, bias_ref, table_ref, qkv_ref, out_ref, stat_ref):
    half = ROTARY // 2
    cos, sin, pos = table_ref[0, :half], table_ref[0, half:ROTARY], table_ref[0, ROTARY:]
    parts = []
    for i in range(3):
        v = kept_ref[i, 0].astype(f32) + got_ref[i, 0].astype(f32) + bias_ref[i, 0]
        if i < 2:
            a, b = v[:half], v[half:ROTARY]
            v = jnp.concatenate([a * cos - b * sin, b * cos + a * sin, v[ROTARY:]], axis=0)
        v = v.astype(bf16)
        qkv_ref[i, 0] = v
        parts.append(v)
    q, k, v = parts
    scores = dot(k, q, FIRST) * score_scale
    scores = jnp.where(pos.T[:, :1] <= pos[:1], scores, masked_score)
    peak = jnp.max(scores, axis=0, keepdims=True)
    e = jnp.exp(scores - peak)
    total = jnp.sum(e, axis=0, keepdims=True)
    p = (e / total).astype(bf16)
    out_ref[0] = dot(v, p, PLAIN).astype(bf16)
    stat_ref[0, 0] = jnp.concatenate([peak, total], axis=0)


def attend(kept, got, bias, table):
    _, heads, hd, t = kept.shape
    seqs, _, seq = table.shape
    big = pl.BlockSpec((3, 1, hd, seq), lambda s, h: (0, h, 0, s))
    table_spec = pl.BlockSpec((1, table.shape[1], seq), lambda s, h: (s, 0, 0))
    stat = pl.BlockSpec((1, 1, 2, seq), lambda s, h: (s, h, 0, 0))
    return pl.pallas_call(
        attend_kernel,
        grid=(seqs, heads),
        in_specs=[
            big,
            big,
            pl.BlockSpec((3, 1, hd, 1), lambda s, h: (0, h, 0, 0)),
            table_spec,
        ],
        out_specs=[big, pl.BlockSpec((1, hd, seq), lambda s, h: (h, 0, s)), stat],
        out_shape=[
            jax.ShapeDtypeStruct((3, heads, hd, t), bf16),
            jax.ShapeDtypeStruct((heads, hd, t), bf16),
            jax.ShapeDtypeStruct((seqs, heads, 2, seq), f32),
        ],
        compiler_params=pltpu.CompilerParams(vmem_limit_bytes=32 * 1024 * 1024),
        cost_estimate=SMALL,
    )(kept, got, bias, table)


def attend_back_kernel(qkv_ref, dout_ref, stat_ref, table_ref, out_ref):
    half = ROTARY // 2
    cos, sin, pos = table_ref[0, :half], table_ref[0, half:ROTARY], table_ref[0, ROTARY:]
    q, k, v = qkv_ref[0, 0], qkv_ref[1, 0], qkv_ref[2, 0]
    dout = dout_ref[0]
    scores = dot(k, q, FIRST) * score_scale
    scores = jnp.where(pos.T[:, :1] <= pos[:1], scores, masked_score)
    p = jnp.exp(scores - stat_ref[0, 0, :1]) / stat_ref[0, 0, 1:]
    dp = dot(v, dout, FIRST)
    inner = jnp.sum(p * dp, axis=0, keepdims=True)
    ds = (p * (dp - inner)).astype(bf16)

    def back(x):
        a, b = x[:half], x[half:ROTARY]
        return jnp.concatenate([a * cos + b * sin, b * cos - a * sin, x[ROTARY:]], axis=0)

    out_ref[0, 0] = back(dot(k, ds, PLAIN) * score_scale).astype(bf16)
    out_ref[1, 0] = back(dot(q, ds, LAST) * score_scale).astype(bf16)
    out_ref[2, 0] = dot(dout, p.astype(bf16), LAST).astype(bf16)


def attend_back(qkv, dout, stats, table):
    _, heads, hd, t = qkv.shape
    seqs, _, seq = table.shape
    big = pl.BlockSpec((3, 1, hd, seq), lambda s, h: (0, h, 0, s))
    table_spec = pl.BlockSpec((1, table.shape[1], seq), lambda s, h: (s, 0, 0))
    stat = pl.BlockSpec((1, 1, 2, seq), lambda s, h: (s, h, 0, 0))
    return pl.pallas_call(
        attend_back_kernel,
        grid=(seqs, heads),
        in_specs=[
            big,
            pl.BlockSpec((1, hd, seq), lambda s, h: (h, 0, s)),
            stat,
            table_spec,
        ],
        out_specs=big,
        out_shape=jax.ShapeDtypeStruct((3, heads, hd, t), bf16),
        compiler_params=pltpu.CompilerParams(vmem_limit_bytes=32 * 1024 * 1024),
        cost_estimate=SMALL,
    )(qkv, dout, stats, table)


def body(
    tokens,
    cotangent,
    span_order,
    w_qkv,
    w_out,
    w_up,
    w_down,
    norm_params,
    m_qkv,
    v_qkv,
    m_out,
    v_out,
    m_up,
    v_up,
    m_down,
    v_down,
    m_norm,
    v_norm,
):
    at = Plane()
    do = Order()
    reps = RepSum(do)
    width = tokens.shape[3]
    rows = tokens.shape[1]
    S, Y, nb = at.s_size, at.y_size, at.blocks
    plane = ("ctx", "shard")
    blk = width // nb
    ffb = FF // nb
    heads = blk // HEAD_DIM
    seq = rows * at.ctx_size
    T = S * seq
    H = T // 2
    first = at.c == 0
    core = at.c.reshape(1)
    my_block = at.ctx * S + at.s
    halves = (slice(0, H), slice(H, T))
    seqs = (slice(0, S // 2), slice(S // 2, S))

    def pick(x, axis, which):
        return lax.dynamic_index_in_dim(x, which, axis, keepdims=False)

    def in_order(mine, theirs, axis):
        return jnp.stack([jnp.where(first, mine, theirs), jnp.where(first, theirs, mine)], axis=axis)

    def join(a, b):
        return jnp.concatenate([a, b], axis=0)

    def lanes(a, b):
        return jnp.concatenate([a, b], axis=1)

    def gather_steps(parts, pre):
        n = len(at.steps(False))
        state = {"parts": list(parts)}

        def start(i, after=None):
            if after is not None:
                state["parts"], _ = lax.optimization_barrier((state["parts"], after))
            state["got"] = []
            state["at"] = []
            for k in range(2):
                axis, step = list(reversed(at.steps(bool(k))))[i]
                state["at"].append((axis, step))
                state["got"].append(at.along(state["parts"][k], axis, step))

        def finish():
            def put(parts, got):
                out = []
                for k in range(2):
                    axis, step = state["at"][k]
                    ax = {"y": 0, "s": 1}[axis]
                    low = (at.index(axis) // step) % 2 == 0
                    a, b = parts[k], got[k]
                    out.append(jnp.concatenate([jnp.where(low, a, b), jnp.where(low, b, a)], ax))
                return out

            state["parts"] = do(put, state["parts"], state["got"])

        def result():
            ys, ss = Y // 2, S // 2
            bits = jnp.stack([at.y // ys, at.s // ss, jnp.int32(ys), jnp.int32(ss)]).astype(jnp.int32)
            return do(lambda p, g: last_step(p, g, bits, pre, Y, S), state["parts"], state["got"])

        return n, start, finish, result if pre else state

    x_rows = tokens.reshape(rows, width)
    order = span_order.reshape(-1).astype(f32)
    span = rows // 2

    def pack(x, order):
        xf = x.astype(f32)
        mean = jnp.mean(xf, axis=1)
        centred = xf - mean[:, None]
        inv = lax.rsqrt(jnp.mean(centred * centred, axis=1) + eps_norm)
        mine = lax.dynamic_slice_in_dim(order, 2 * at.ctx, 2)
        place = jnp.repeat(mine, span)
        terms = []
        for v in (mean, inv):
            for _ in range(3):
                t = lax.reduce_precision(v, 8, 7)
                terms.append(t)
                v = v - t
        extra = jnp.stack(terms + [place] + [jnp.zeros_like(place)] * 9).astype(bf16)
        blocks = x.T.reshape(nb, blk, rows)
        return jnp.concatenate([blocks, jnp.broadcast_to(extra[None], (nb, 16, rows))], axis=1)

    packed = do(pack, x_rows, order)
    got = lax.all_to_all(packed, plane, split_axis=0, concat_axis=0, tiled=True)

    def chip_rows(w, lead, unit, count):
        mine, theirs = do(lambda w: split_columns(w, core, lead, unit, count), w)
        return mine, at.core(theirs)

    wq_parts = chip_rows(w_qkv, 0, S * blk, 3 * Y)
    norm_cols = norm_params.reshape(7, nb, blk).transpose(1, 2, 0)
    own_cols = pick(norm_cols, 0, my_block)
    other_cols = pick(norm_cols, 0, (at.ctx ^ 1) * S + at.s)
    pair_cols = join(own_cols, other_cols)
    bias = own_cols[:, 4:7].T.reshape(3, heads, HEAD_DIM, 1)
    spot = jnp.stack([at.y, at.s])

    def cut_weights(parts, pre, unit, flip):
        return do(lambda a, b: arrange(a, b, spot, pre, Y, S, unit, flip), *parts)

    wq_cut = [cut_weights(wq_parts, 3, blk, bool(k)) for k in range(2)]

    def columns(got):
        x = got.reshape(at.ctx_size, S, blk + 16, rows).transpose(2, 1, 0, 3).reshape(blk + 16, T)
        x_own, extra = x[:blk], x[blk:].astype(f32)
        mean = extra[0:1] + extra[1:2] + extra[2:3]
        inv = extra[3:4] + extra[4:5] + extra[5:6]
        return x_own, mean, inv, extra[6:7]

    x_own, mean1, inv1, place = do(columns, got)
    x_other = at.core(x_own)
    cot = cotangent.reshape(2, 1, 1, rows // 2, width)
    cot_n, cot_start, cot_finish, cot_state = gather_steps([cot[0], cot[1]], 0)
    cot_start(0, x_own)

    def first_norm(mine, theirs, mean, inv, cols):
        x = join(mine, theirs).astype(f32)
        return ((x - mean) * inv * cols[:, 0:1] + cols[:, 1:2]).astype(bf16)

    xn1 = do(first_norm, x_own, x_other, mean1, inv1, pair_cols)

    def send_products(cut, xs):
        got, kept = [], []
        for k in range(2):
            axis, step = at.steps(bool(k))[0]
            p = do(lambda w, x: dot(w, x, PLAIN).astype(bf16), cut[k][0], xs[k])
            got.append(at.along(p, axis, step))
        for k in range(2):
            kept.append(do(lambda w, x: dot(w, x, PLAIN).astype(bf16), cut[k][1], xs[k]))
        return list(zip(kept, got))

    def scatter_rest(pairs):
        for i in range(1, len(at.steps(False))):
            out = []
            for k in range(2):
                axis, step = at.steps(bool(k))[i]
                bit = (at.index(axis) // step) % 2
                send, kept = do(lambda a, b: add_split(a, b, bit.reshape(1)), *pairs[k])
                out.append((kept, at.along(send, axis, step)))
            pairs = out
        return pairs

    flying = send_products(wq_cut, [xn1[:, h] for h in halves])

    for i in range(1, cot_n):
        cot_finish()
        cot_start(i)

    wo_parts = chip_rows(w_out, 0, S * blk, Y)
    wg_parts = chip_rows(w_up, 0, S * ffb, Y)
    wu_parts = chip_rows(w_up, Y, S * ffb, Y)
    wo_cut = [cut_weights(wo_parts, 1, blk, bool(k)) for k in range(2)]

    def positions(place):
        pos = place.reshape(S, seq) * span + (jnp.arange(seq) % span).astype(f32)[None, :]
        prow = pos.reshape(S, 1, seq)
        exponent = jnp.arange(ROTARY // 2, dtype=f32)
        inverse = 10000.0 ** (-2.0 * exponent / ROTARY)
        angles = prow * inverse[None, :, None]
        return jnp.concatenate([jnp.cos(angles), jnp.sin(angles), jnp.broadcast_to(prow, (S, 8, seq))], axis=1)

    table = do(positions, place)
    flying = scatter_rest(flying)

    cot_finish()
    cot_parts = cot_state["parts"]
    cot_theirs = [at.core(p) for p in cot_parts]

    qkvs, attns, attn_got, stats = [], [], [], []
    for k in range(2):
        shape = (3, heads, HEAD_DIM, H)
        qkv, attn, stat = do(attend, flying[k][0].reshape(shape), flying[k][1].reshape(shape), bias, table[seqs[k]])
        qkvs.append(qkv)
        attns.append(attn.reshape(blk, H))
        attn_got.append(at.core(attns[k]))
        stats.append(stat)
    pairs = [do(join, attns[k], attn_got[k]) for k in range(2)]
    flying = send_products(wo_cut, pairs)
    wg_cut = cut_weights(wg_parts, 1, ffb, False)
    wu_cut = cut_weights(wu_parts, 1, ffb, True)

    def gain_products(wg, wu, cols):
        terms = []
        for v in (cols[:, 2], cols[:, 3]):
            t = lax.reduce_precision(v, 8, 7)
            terms += [t, v - t]
        terms = jnp.stack(terms).astype(bf16)
        out = []
        for mine, theirs in (wg, wu):
            p = dot(terms[:, :blk], mine, LAST) + dot(terms[:, blk:], theirs, LAST)
            out.append(jnp.stack([p[0] + p[1], p[2] + p[3]]).reshape(2, Y, S, ffb))
        return jnp.concatenate(out, axis=0)

    gains = do(gain_products, wg_parts, wu_parts, pair_cols)
    gain_steps = list(at.steps(False))

    def gain_step(gains):
        axis, step = gain_steps.pop(0)
        ax = {"y": 1, "s": 2}[axis]
        bit = (at.index(axis) // step) % 2
        send = lax.dynamic_slice_in_dim(gains, (1 - bit) * step, step, ax)
        kept = lax.dynamic_slice_in_dim(gains, bit * step, step, ax)
        return kept, at.along(send, axis, step)

    flying = scatter_rest(flying)
    def residual(x, a0, b0, a1, b1):
        a, b = lanes(a0, a1), lanes(b0, b1)
        hidden = x.astype(f32) + (a.astype(f32) + b.astype(f32))
        local_mean = jnp.mean(hidden, axis=0, keepdims=True)
        dev = hidden - local_mean
        return hidden, join(local_mean, jnp.sum(dev * dev, axis=0, keepdims=True))

    hidden, moments = do(residual, x_own, *flying[0], *flying[1])
    count = blk
    for axis, step in at.steps(False) + [("core", 1)]:
        other = at.core(moments) if axis == "core" else at.along(moments, axis, step)

        def merge(a, b):
            gap = a[0:1] - b[0:1]
            return join(0.5 * (a[0:1] + b[0:1]), a[1:2] + b[1:2] + gap * gap * (count / 2.0))

        moments = do(merge, moments, other)
        count *= 2

    def second_norm(hidden, moments, cols):
        inv2 = lax.rsqrt(moments[1:2] / width + eps_norm)
        z2 = (hidden - moments[0:1]) * inv2
        return (z2 * cols[:, 2:3] + cols[:, 3:4]).astype(bf16), z2, inv2

    gains = gain_step(gains)
    xn2_own, z2, inv2 = do(second_norm, hidden, moments, own_cols)
    xn2 = do(join, xn2_own, at.core(xn2_own))

    flying = send_products([wg_cut, wu_cut], [xn2, xn2])

    wd_own = do(cast, w_down)
    wg = do(stack_turned, *wg_parts)
    wu = do(stack_turned, *wu_parts)
    cot_all = do(lambda a, b: token_rows(a, b, core), cot_parts, cot_theirs)
    grad_act = do(lambda w, c: mm(w, c, LAST, f32, tn=256), wd_own, cot_all)
    cot_cols = do(lambda c: own_columns(c, my_block.reshape(1), blk), cot_all)
    wo_own = do(cast, w_out)
    wq = do(stack_turned, *wq_parts)
    gains = do(lambda a, b: a + b, *gains)
    while gain_steps:
        gains = do(lambda a, b: a + b, *gain_step(gains))
    gains = do(lambda g: g.reshape(4, ffb).T, gains)
    flying = scatter_rest(flying)

    gate0, gate1, up0, up1, act, sums = do(gated, *flying[0], *flying[1], grad_act, gains)

    def parts_of(count, want):
        return max(n for n in range(1, want + 1) if count % (16 * n) == 0)

    def even(count, want):
        n = parts_of(count, want)
        return [(k * (count // n), count // n) for k in range(n)]

    down_rows, up_rows = even(ffb, 2), [(0, blk)]

    def push_pairs(name, g, rows):
        for k, (at_row, count) in enumerate(rows):
            reps.push((name, "theirs", k), g[blk + at_row : blk + at_row + count])
            reps.push((name, "mine", k), g[at_row : at_row + count])

    results = {"down": None, "out": None, "up": None, "qkv": None}
    states = {
        "down": (w_down, m_down, v_down),
        "out": (w_out, m_out, v_out),
        "up": (w_up, m_up, v_up),
        "qkv": (w_qkv, m_qkv, v_qkv),
    }
    rates = {"down": 0.02, "out": 0.2, "up": 0.03, "qkv": 0.03}

    def adam(name, grads, row_first, lead, unit, rb):
        results[name] = do(
            lambda s, g, prev: adam_part(s, g, core, rates[name], prev, row_first, lead, unit, rb),
            states[name],
            grads,
            results[name],
        )

    jobs = []
    for k, (at_row, count) in enumerate(down_rows):
        jobs.append(("down", [("down", k)], at_row, 0, count, 1024))
    for name, lead in (("gate", 0), ("up", Y)):
        for k, (at_row, count) in enumerate(up_rows):
            jobs.append(("up", [(name, "mine", k), (name, "theirs", k)], at_row, lead, count, S * ffb))
    for k in range(2):
        jobs.append(("out", [("out", k)], 0, k, blk, width // 2))
    for third in (2, 1, 0):
        jobs.append(("qkv", [(third, 0), (third, 1, "theirs")], 0, third * Y, blk, S * blk))
    received = {}

    def update(limit):
        for name in list(reps.done):
            if name in ("out", 0, 1, 2):
                g = reps.done.pop(name)
                half = g.shape[0] // 2
                reps.done[(name, 0)] = g[:half]
                reps.done[(name, 1) if name == "out" else (name, 1, "theirs")] = g[half:]
        for name in list(reps.done):
            if "theirs" in name and name not in received:
                received[name] = at.core(reps.done[name])
        while jobs and limit and all(k in reps.done for k in jobs[0][1]):
            name, needs, at_row, lead, count, unit = jobs.pop(0)
            rb = max(n for n in range(8, min(count, 176) + 1, 8) if count % n == 0 and at_row % n == 0)
            adam(name, [received[k] if "theirs" in k else reps.done[k] for k in needs], at_row, lead, unit, rb)
            limit -= 1

    def ticks(n):
        for _ in range(n):
            reps.tick()

    wide = 2 * FF // 8

    def quarter_heads(x):
        return [x[:, h][None, None] for h in halves]

    n, start, finish, gate_all = gather_steps([gate0[None, None], gate1[None, None]], 1)
    start(0)
    g_down = do(lambda a, c: mm(a, c, PLAIN, bf16, tn=512), act, cot_all)
    for k, (at_row, count) in enumerate(down_rows):
        reps.push(("down", k), g_down[at_row : at_row + count])
    ticks(1)

    steps2 = at.steps(False) + [("core", 1)]

    def sum_send(sums, axis, step):
        return at.core(sums) if axis == "core" else at.along(sums, axis, step)

    def sum_step(sums, axis, step):
        return do(lambda a, b: a + b, sums, sum_send(sums, axis, step))

    tiny = list(steps2)
    sums_got = sum_send(sums, *tiny.pop(0))
    for i in range(1, n):
        finish()
        sums = do(lambda a, b: a + b, sums, sums_got)
        sums_got = sum_send(sums, *tiny.pop(0))
        start(i, sums)
        ticks(1)
    n, start_up, finish_up, up_all = gather_steps([up0[None, None], up1[None, None]], 1)
    ggate_all = gate_all().reshape(Y * S * ffb, T)
    sums = do(lambda a, b: a + b, sums, sums_got)
    start_up(0, sums)
    while tiny:
        sums = sum_step(sums, *tiny.pop(0))
    g_gate = do(lambda x, g: mm(x, g, LAST, bf16, tn=wide), xn2, ggate_all)
    push_pairs("gate", g_gate, up_rows)
    finish_up()
    for i in range(1, n):
        start_up(i)
        if i == 1:
            part_gate = do(lambda w, g: mm(w, g, PLAIN, f32, tn=256), wg, ggate_all)
            out_part = do(lambda w, a: mm(w, a, FIRST, bf16, tm=512), wd_own, act)
            ticks(1)
        if i < n - 1:
            finish_up()
    gup_all = up_all().reshape(Y * S * ffb, T)
    part = do(lambda w, g, p: dot(w, g, PLAIN) + p, wu, gup_all, part_gate)
    part_theirs = at.core(part[blk:])

    def branch(a, b, cot, z, scale, gain, sums):
        gxn2 = a + b
        e = gxn2 * gain
        grad_hidden = cot.astype(f32) + scale * (e - sums[0:1] / width - z * (sums[1:2] / width))
        return grad_hidden.astype(bf16), grad_hidden, gxn2

    grad_branch, grad_hidden, gxn2 = do(
        branch, part[:blk], part_theirs, cot_cols, z2, inv2, own_cols[:, 2:3], sums
    )
    n, start, finish, branch_all = gather_steps(quarter_heads(grad_branch), 1)
    start(0)
    g_up = do(lambda x, g: mm(x, g, LAST, bf16, tn=wide), xn2, gup_all)
    push_pairs("up", g_up, up_rows)
    finish()
    for i in range(1, n):
        start(i)
        if i == 1:
            ticks(1)
        if i < n - 1:
            finish()
    gbr_c = branch_all()[0]
    gbr_o = at.core(gbr_c)
    gbr = do(lambda a, b: in_order(a, b, 1).reshape(width, T), gbr_c, gbr_o)
    grad_attn = do(lambda w, g: dot(w, g, PLAIN).astype(bf16), wo_own, gbr)

    gqkvs = []
    for k in range(2):
        dout = grad_attn[:, halves[k]].reshape(heads, HEAD_DIM, H)
        gqkvs.append(do(attend_back, qkvs[k], dout, stats[k], table[seqs[k]]).reshape(3, blk, H))
    n, start, finish, gqkv_done = gather_steps([g.reshape(1, 1, 3 * blk, H) for g in gqkvs], 3)
    start(0)
    attn = lanes(*attns)
    g_out = do(
        lambda a, g: join(*[mm(a, g[k * width // 2 : (k + 1) * width // 2], LAST, bf16, tn=512) for k in range(2)]),
        attn,
        gbr,
    )
    reps.push("out", g_out)
    update(1)
    ticks(1)
    finish()
    for i in range(1, n):
        start(i)
        if i == 1:
            update(1)
            ticks(1)
        if i < n - 1:
            finish()
    gqkv = gqkv_done().reshape(3, Y * S * blk, T)
    out_split = out_part.reshape(Y, 2, S * blk, T)
    out_kept = pick(out_split, 1, at.c).reshape(-1, T)
    out_got = at.core(pick(out_split, 1, 1 - at.c).reshape(-1, T))

    def out_step(axis, step):
        bit = (at.index(axis) // step) % 2
        send, kept = do(lambda a, b: add_split(a, b, bit.reshape(1)), out_kept, out_got)
        return kept, at.along(send, axis, step)

    out_steps = at.steps(True)
    g = do(lambda x, g: mm(x, g, LAST, bf16, tn=512), xn1, gqkv[2])
    reps.push(2, g)
    ticks(1)
    for third in (1, 0):
        g = do(lambda x, g: mm(x, g, LAST, bf16, tn=512), xn1, gqkv[third])
        reps.push(third, g)
    part = do(lambda w, g: mm(w, g, PLAIN, f32, tn=256), wq, gqkv.reshape(3 * Y * S * blk, T))
    part_theirs = at.core(part[blk:])

    def first_back(a, b, x, mean, inv, gain, gxn2, z2, gqkv0, gqkv1):
        gxn1 = a + b
        z1 = (x.astype(f32) - mean) * inv
        e = gxn1 * gain
        sums = join(jnp.sum(e, axis=0, keepdims=True), jnp.sum(e * z1, axis=0, keepdims=True))
        small = jnp.concatenate(
            [
                jnp.sum(gxn1 * z1, axis=1)[None],
                jnp.sum(gxn1, axis=1)[None],
                jnp.sum(gxn2 * z2, axis=1)[None],
                jnp.sum(gxn2, axis=1)[None],
                jnp.sum(gqkv0.astype(f32), axis=2) + jnp.sum(gqkv1.astype(f32), axis=2),
            ],
            axis=0,
        )
        return sums, small, gxn1, z1

    sums, small, gxn1, z1 = do(
        first_back, part[:blk], part_theirs, x_own, mean1, inv1, own_cols[:, 0:1], gxn2, z2, *gqkvs
    )
    for axis, step in steps2:
        sums = sum_step(sums, axis, step)
    ticks(1)
    input_grad = do(
        lambda h, grad, z, scale, gain, sums: (
            h + scale * (grad * gain - sums[0:1] / width - z * (sums[1:2] / width))
        ).astype(bf16),
        grad_hidden,
        gxn1,
        z1,
        inv1,
        own_cols[:, 0:1],
        sums,
    )

    def to_rows(cols):
        split = do(lambda c: c.reshape(blk, S, at.ctx_size, rows).transpose(2, 1, 0, 3).reshape(nb, blk, rows), cols)
        got = lax.all_to_all(split, plane, split_axis=0, concat_axis=0, tiled=True)
        return do(lambda g: g.reshape(width, rows).T, got)

    input_rows = to_rows(input_grad).astype(f32)
    steps_rep = []
    step = 1
    while step < lax.axis_size("rep"):
        steps_rep.append(step)
        step *= 2

    def small_step():
        nonlocal small
        small = getattr(reps, "kept", small)
        k = steps_rep.pop(0)
        other = lax.ppermute(small, "rep", [(i, i ^ k) for i in range(lax.axis_size("rep"))])
        small = do(lambda a, b: a + b, small, other)
        return small

    out_kept, out_got = out_step(*out_steps[0])
    reps.tick(small_step)
    update(1)
    for axis, step in out_steps[1:]:
        out_kept, out_got = out_step(axis, step)
    reps.tick(small_step)
    sent = do(lambda s: jnp.broadcast_to(s.reshape(1, 7, blk), (nb, 7, blk)), reps.kept)
    small_all = lax.all_to_all(sent, plane, split_axis=0, concat_axis=0, tiled=True)

    def norm_update(every, *a):
        return adam_update(*a, every.transpose(1, 0, 2).reshape(7, width), 0.3, 0.0)

    mn, vn, wn = do(norm_update, small_all, norm_params, m_norm, v_norm)
    update(2)
    ticks(1)
    update(1)
    out_cols = do(
        lambda h, a, b: (h + (a.astype(f32) + b.astype(f32))).astype(bf16), hidden, out_kept, out_got
    )
    block_output = to_rows(out_cols)
    while reps.busy():
        reps.tick()
        update(2)
    update(len(jobs))
    return (
        (block_output.reshape(tokens.shape), input_rows.reshape(tokens.shape))
        + tuple(results["qkv"])
        + tuple(results["out"])
        + tuple(results["up"])
        + tuple(results["down"])
        + (mn, vn, wn)
    )


def solution(mesh):
    tok = P("rep", "ctx", "shard", None)
    row = P(("ctx", "shard"), None)
    placed = (tok, tok, P("rep", "shard", None)) + (row,) * 4 + (P(),) + (row,) * 8 + (P(), P())
    return jax.shard_map(
        body,
        mesh=mesh,
        in_specs=placed,
        out_specs=(tok, tok) + (row,) * 12 + (P(),) * 3,
        check_vma=False,
    )
```

profile of v0, /device:TPU:0, one launch (start us, length us, event | category | flops | bytes accessed | tf_op | source)
XLA Modules:
  0.0 879.7 jit_solution(14072970349448386279)
XLA Ops:
  12.9 4.8 all-to-all-start
  64.8 14.9 %collective-permute-done.5.b_ref.d_ref = bf16[1536,512]{1,0:T(8,128)(2,1)} collective-permute-done((bf16[1536,512]{1,0:T(8,128)(2,1)}, bf16[1536,512]{1,0:T(8,128)(2,1)}, u32[]{:S(2)}, u32[]{:S(2)}) %collective-permute-start.5) | collective-permute-done | bytes 1572896 | tf_op jit(solution)/shard_map/ppermute | solution.py:62
  96.1 12.6 %collective-permute-done.6 = bf16[768,512]{1,0:T(8,128)(2,1)S(1)} collective-permute-done((bf16[768,512]{1,0:T(8,128)(2,1)S(1)}, bf16[768,512]{1,0:T(8,128)(2,1)S(1)}, u32[]{:S(2)}, u32[]{:S(2)}) %collective-permute-start.6) | collective-permute-done | bytes 786464 | tf_op jit(solution)/shard_map/ppermute | solution.py:61
  141.3 13.2 %shard_map.318 = (bf16[1408,512]{1,0:T(8,128)(2,1)S(1)}, bf16[1408,512]{1,0:T(8,128)(2,1)S(1)}) custom-call(s32[2]{0:T(128)S(1)} %pad_add_fusion.at_ref, bf16[2816,256]{1,0:T(8,128)(2,1)S(1)} %copy-done.14, bf16[2816,256]{1,0:T(8,128)(2,1)S(1)} %collective-permute-done.15.b_ref.d_ref, bf16[2816,256]{1,0:T(8,128)(2,1)S(1)} %copy-done.14, ...), custom_call_target="tpu_custom_call" | custom-call | flops 1024 | bytes 1024 | tf_op jit(solution)/shard_map/pallas_call | solution.py:352
  168.5 5.0 pad_maximum_fusion.3
  179.7 5.6 collective-permute-done.18
  214.8 5.0 convolution_convert_fusion.1.a_ref.c_ref
  231.7 5.9 shard_map.324.b_ref.x_ref
  239.7 5.5 shard_map.325.grad_ref
  255.3 11.8 %collective-permute-done.24 = f32[4,2,1,704]{3,0,2,1:T(4,128)S(1)} collective-permute-done((f32[4,2,1,704]{3,0,2,1:T(4,128)S(1)}, f32[4,2,1,704]{3,0,2,1:T(4,128)S(1)}, u32[]{:S(2)}, u32[]{:S(2)}) %collective-permute-start.24) | collective-permute-done | bytes 22560 | tf_op jit(solution)/shard_map/ppermute | solution.py:62
  270.9 8.8 collective-permute-done.27
  290.4 29.5 %collective-permute-done.30.ub_ref = bf16[704,1024]{1,0:T(8,128)(2,1)S(1)} collective-permute-done((bf16[704,1024]{1,0:T(8,128)(2,1)S(1)}, bf16[704,1024]{1,0:T(8,128)(2,1)S(1)}, u32[]{:S(2)}, u32[]{:S(2)}) %collective-permute-start.30) | collective-permute-done | bytes 1441824 | tf_op jit(solution)/shard_map/ppermute | solution.py:62
  321.8 7.5 shard_map.331
  334.2 5.8 shard_map.332
  350.3 22.4 %collective-permute-done.36 = bf16[352,2048]{1,0:T(8,128)(2,1)S(1)} collective-permute-done((bf16[352,2048]{1,0:T(8,128)(2,1)S(1)}, bf16[352,2048]{1,0:T(8,128)(2,1)S(1)}, u32[]{:S(2)}, u32[]{:S(2)}) %collective-permute-start.36) | collective-permute-done | bytes 1441824 | tf_op jit(solution)/shard_map/ppermute | solution.py:199
  385.9 6.5 collective-permute-start.44
  392.4 5.7 shard_map.334
  401.7 5.8 shard_map.335
  407.6 5.3 shard_map.336
  412.9 9.9 %collective-permute-done.44 = bf16[352,2048]{1,0:T(8,128)(2,1)} collective-permute-done((bf16[352,2048]{1,0:T(8,128)(2,1)}, bf16[352,2048]{1,0:T(8,128)(2,1)}, u32[]{:S(2)}, u32[]{:S(2)}) %collective-permute-start.44) | collective-permute-done | bytes 1441824 | tf_op jit(solution)/shard_map/ppermute | solution.py:199
  426.3 5.5 collective-permute-done.43.got1_ref
  432.4 5.2 shard_map.337
  437.6 5.2 convolution_add_fusion.2
  456.3 5.8 shard_map.338
  463.9 18.0 %collective-permute-done.52 = bf16[352,2048]{1,0:T(8,128)(2,1)S(1)} collective-permute-done((bf16[352,2048]{1,0:T(8,128)(2,1)S(1)}, bf16[352,2048]{1,0:T(8,128)(2,1)S(1)}, u32[]{:S(2)}, u32[]{:S(2)}) %collective-permute-start.52) | collective-permute-done | bytes 1441824 | tf_op jit(solution)/shard_map/ppermute | solution.py:202
  486.4 9.9 %collective-permute-done.50.got1_ref = bf16[1,2,256,512]{3,2,1,0:T(8,128)(2,1)S(1)} collective-permute-done((bf16[1,2,256,512]{3,2,1,0:T(8,128)(2,1)S(1)}, bf16[1,2,256,512]{3,2,1,0:T(8,128)(2,1)S(1)}, u32[]{:S(2)}, u32[]{:S(2)}) %collective-permute-start.50) | collective-permute-done | bytes 524320 | tf_op jit(solution)/shard_map/ppermute | solution.py:61
  506.8 7.2 collective-permute-start.57
  520.1 5.4 shard_map.340
  525.5 5.5 shard_map.341
  536.9 7.6 shard_map.344
  559.2 8.1 shard_map.345
  567.2 13.2 %collective-permute-done.62 = bf16[256,2816]{1,0:T(8,128)(2,1)S(1)} collective-permute-done((bf16[256,2816]{1,0:T(8,128)(2,1)S(1)}, bf16[256,2816]{1,0:T(8,128)(2,1)S(1)}, u32[]{:S(2)}, u32[]{:S(2)}) %collective-permute-start.62) | collective-permute-done | bytes 1441824 | tf_op jit(solution)/shard_map/ppermute | solution.py:194
  584.0 5.8 collective-permute-start.64
  593.1 9.1 %shard_map.346 = bf16[3,2,2,256,1024]{4,3,2,1,0:T(8,128)(2,1)} custom-call(s32[4]{0:T(128)S(1)} %pad_add_fusion.1.bits_ref, bf16[2,1,768,512]{3,2,1,0:T(8,128)(2,1)S(1)} %pad_maximum_fusion.1.own0_ref, bf16[2,1,768,512]{3,2,1,0:T(8,128)(2,1)S(1)} %collective-permute-done.60.got0_ref, bf16[1,2,768,512]{3,2,1,0:T(8,128)(2,1)S(1)} %pad_maximum_fusion.2.own1_ref, ...), custom_call_target="tpu_custom_call" | custom-call | flops 1024 | bytes 1024 | tf_op jit(solution)/shard_map/pallas_call | solution.py:411
  608.2 12.0 %collective-permute-done.64 = bf16[256,2816]{1,0:T(8,128)(2,1)S(1)} collective-permute-done((bf16[256,2816]{1,0:T(8,128)(2,1)}, bf16[256,2816]{1,0:T(8,128)(2,1)S(1)}, u32[]{:S(2)}, u32[]{:S(2)}) %collective-permute-start.64) | collective-permute-done | bytes 1441824 | tf_op jit(solution)/shard_map/ppermute | solution.py:194
  626.2 6.0 shard_map.350
  638.4 8.5 collective-permute-start.70
  661.6 8.3 collective-permute-done.70
  681.6 10.9 %collective-permute-start.76 = (bf16[512,1024]{1,0:T(8,128)(2,1)}, bf16[512,1024]{1,0:T(8,128)(2,1)}, u32[]{:S(2)}, u32[]{:S(2)}) collective-permute-start(bf16[512,1024]{1,0:T(8,128)(2,1)} %shard_map.347), channel_id=1, source_target_pairs={{0,8},{24,16},{1,9},{25,17},{2,10},{26,18},{3,11},{27,19},{4,12},{... | collective-permute-start | bytes 3145736 | tf_op jit(solution)/shard_map/ppermute | solution.py:199
  701.0 11.8 %collective-permute-start.75 = (f32[7,256]{1,0:T(8,128)S(1)}, f32[7,256]{1,0:T(8,128)S(1)}, u32[]{:S(2)}, u32[]{:S(2)}) collective-permute-start(f32[7,256]{1,0:T(8,128)S(1)} %concatenate.127), channel_id=1, source_target_pairs={{0,8},{8,0},{16,24},{24,16},{1,9},{9,1},{17,25},{25,17},{2,10},{10... | collective-permute-start | bytes 21512 | tf_op jit(solution)/shard_map/ppermute | solution.py:1135
  728.1 13.1 %shard_map.352 = (f32[256,11264]{1,0:T(8,128)}, f32[256,11264]{1,0:T(8,128)}, f32[256,11264]{1,0:T(8,128)}) custom-call(s32[1]{0:T(128)} %bitcast.8.core_ref, f32[256,11264]{1,0:T(8,128)} %w_ref.9, f32[256,11264]{1,0:T(8,128)} %m_ref.3, f32[256,11264]{1,0:T(8,128)} %v_ref.3, bf16[256,2816]{1,0:T(8,128)(2,1)S(1)} %broadcast_select_fusion.3.refs_0_, ...), custom_call_target="tpu_custom_call" | custom-call | flops 1024 | bytes 1024 | tf_op jit(solution)/shard_map/pallas_call | solution.py:522
  764.4 14.5 %shard_map.354 = (f32[256,11264]{1,0:T(8,128)}, f32[256,11264]{1,0:T(8,128)}, f32[256,11264]{1,0:T(8,128)}) custom-call(s32[1]{0:T(128)} %bitcast.8.core_ref, f32[256,11264]{1,0:T(8,128)} %w_ref.9, f32[256,11264]{1,0:T(8,128)} %m_ref.3, f32[256,11264]{1,0:T(8,128)} %v_ref.3, ...), custom_call_target="tpu_custom_call", output_to_operand_aliasing={{0}: (6, {}), {1}: (7, {}), {2}: (8, {})} | custom-call | flops 1024 | bytes 1024 | tf_op jit(solution)/shard_map/pallas_call | solution.py:522
  791.2 20.6 %collective-permute-done.86 = bf16[512,1024]{1,0:T(8,128)(2,1)S(1)} collective-permute-done((bf16[512,1024]{1,0:T(8,128)(2,1)S(1)}, bf16[512,1024]{1,0:T(8,128)(2,1)S(1)}, u32[]{:S(2)}, u32[]{:S(2)}) %collective-permute-start.86) | collective-permute-done | bytes 1048608 | tf_op jit(solution)/shard_map/ppermute | solution.py:202
  819.2 11.8 %all_to_all.20 = bf16[8,256,128]{2,1,0:T(8,128)(2,1)S(1)} all-to-all(bf16[8,256,128]{2,1,0:T(8,128)(2,1)S(1)} %bitcast.207), channel_id=1, replica_groups=mesh['rep'=4,'ctx'=4,'shard'=2] {'ctx','shard'}, dimensions={0} | all-to-all | bytes 1048576 | tf_op jit(solution)/shard_map/all_to_all | solution.py:1121
  837.0 6.7 shard_map.357
  843.8 6.7 shard_map.358
  863.8 7.5 all-to-all-done.3
  873.3 6.2 shard_map.359
  (724 shorter events, 428.6 us)
Async XLA Ops:
  42.1 37.6 %collective-permute-start.5 = (bf16[1536,512]{1,0:T(8,128)(2,1)}, bf16[1536,512]{1,0:T(8,128)(2,1)}, u32[]{:S(2)}, u32[]{:S(2)}) collective-permute-start(bf16[1536,512]{1,0:T(8,128)(2,1)} %convolution_convert_fusion.7), channel_id=1, source_target_pairs={{0,1},{1,0},{2,3},{3,2},{4,5},{5,4},{6,7},{7,6},{8,9},{9,8},{10,11... | collective-permute-start | bytes 4718600 | tf_op jit(solution)/shard_map/ppermute | solution.py:62
  44.8 41.0 %collective-permute-start.9 = (bf16[1536,512]{1,0:T(8,128)(2,1)}, bf16[1536,512]{1,0:T(8,128)(2,1)}, u32[]{:S(2)}, u32[]{:S(2)}) collective-permute-start(bf16[1536,512]{1,0:T(8,128)(2,1)} %convolution_convert_fusion.6), channel_id=1, source_target_pairs={{0,4},{2,6},{4,0},{6,2},{1,5},{3,7},{5,1},{7,3},{8,12},{10,14},{12... | collective-permute-start | bytes 4718600 | tf_op jit(solution)/shard_map/ppermute | solution.py:61
  50.3 43.4 %collective-permute-start.7 = (bf16[2,1,64,2048]{3,2,1,0:T(8,128)(2,1)}, bf16[2,1,64,2048]{3,2,1,0:T(8,128)(2,1)}, u32[]{:S(2)}, u32[]{:S(2)}) collective-permute-start(bf16[2,1,64,2048]{3,2,1,0:T(8,128)(2,1)} %pad_maximum_fusion.12), channel_id=1, source_target_pairs={{0,1},{1,0},{2,3},{3,2},{4,5},{5,4},{6,7},{7,6},{8,9},{9,8},{10,11... | collective-permute-start | bytes 1572872 | tf_op jit(solution)/shard_map/ppermute | solution.py:62
  53.6 40.1 %collective-permute-start.8 = (bf16[1,2,64,2048]{3,2,1,0:T(8,128)(2,1)}, bf16[1,2,64,2048]{3,2,1,0:T(8,128)(2,1)}, u32[]{:S(2)}, u32[]{:S(2)}) collective-permute-start(bf16[1,2,64,2048]{3,2,1,0:T(8,128)(2,1)} %pad_maximum_fusion.13), channel_id=1, source_target_pairs={{0,4},{2,6},{4,0},{6,2},{1,5},{3,7},{5,1},{7,3},{8,12},{10,14},{12... | collective-permute-start | bytes 1572872 | tf_op jit(solution)/shard_map/ppermute | solution.py:61
  89.4 29.9 %collective-permute-start.11 = (bf16[768,512]{1,0:T(8,128)(2,1)}, bf16[768,512]{1,0:T(8,128)(2,1)}, u32[]{:S(2)}, u32[]{:S(2)}) collective-permute-start(bf16[768,512]{1,0:T(8,128)(2,1)} %get-tuple-element.519), channel_id=1, source_target_pairs={{0,1},{1,0},{2,3},{3,2},{4,5},{5,4},{6,7},{7,6},{8,9},{9,8},{10,11... | collective-permute-start | bytes 2359304 | tf_op jit(solution)/shard_map/ppermute | solution.py:62
  132.6 41.0 %collective-permute-start.13 = (bf16[512,512]{1,0:T(8,128)(2,1)}, bf16[512,512]{1,0:T(8,128)(2,1)}, u32[]{:S(2)}, u32[]{:S(2)}) collective-permute-start(bf16[512,512]{1,0:T(8,128)(2,1)} %convolution_convert_fusion.11), channel_id=1, source_target_pairs={{0,1},{1,0},{2,3},{3,2},{4,5},{5,4},{6,7},{7,6},{8,9},{9,8},{10,11... | collective-permute-start | bytes 1572872 | tf_op jit(solution)/shard_map/ppermute | solution.py:62
  135.3 40.3 %collective-permute-start.17 = (bf16[512,512]{1,0:T(8,128)(2,1)}, bf16[512,512]{1,0:T(8,128)(2,1)}, u32[]{:S(2)}, u32[]{:S(2)}) collective-permute-start(bf16[512,512]{1,0:T(8,128)(2,1)} %convolution_convert_fusion.10), channel_id=1, source_target_pairs={{0,4},{2,6},{4,0},{6,2},{1,5},{3,7},{5,1},{7,3},{8,12},{10,14},{12... | collective-permute-start | bytes 1572872 | tf_op jit(solution)/shard_map/ppermute | solution.py:61
  201.8 78.7 %collective-permute-start.23 = (bf16[1408,1024]{1,0:T(8,128)(2,1)}, bf16[1408,1024]{1,0:T(8,128)(2,1)}, u32[]{:S(2)}, u32[]{:S(2)}) collective-permute-start(bf16[1408,1024]{1,0:T(8,128)(2,1)} %convolution_convert_fusion.3), channel_id=1, source_target_pairs={{0,1},{1,0},{2,3},{3,2},{4,5},{5,4},{6,7},{7,6},{8,9},{9,8},{10,11... | collective-permute-start | bytes 8650760 | tf_op jit(solution)/shard_map/ppermute | solution.py:62
  206.0 77.4 %collective-permute-start.29 = (bf16[1408,1024]{1,0:T(8,128)(2,1)}, bf16[1408,1024]{1,0:T(8,128)(2,1)}, u32[]{:S(2)}, u32[]{:S(2)}) collective-permute-start(bf16[1408,1024]{1,0:T(8,128)(2,1)} %convolution_convert_fusion.2), channel_id=1, source_target_pairs={{0,4},{2,6},{4,0},{6,2},{1,5},{3,7},{5,1},{7,3},{8,12},{10,14},{12... | collective-permute-start | bytes 8650760 | tf_op jit(solution)/shard_map/ppermute | solution.py:61
  214.2 52.8 %collective-permute-start.24 = (f32[4,2,1,704]{3,0,2,1:T(4,128)S(1)}, f32[4,2,1,704]{3,0,2,1:T(4,128)S(1)}, u32[]{:S(2)}, u32[]{:S(2)}) collective-permute-start(f32[4,2,1,704]{3,0,2,1:T(4,128)S(1)} %copy.134), channel_id=1, source_target_pairs={{0,1},{1,0},{2,3},{3,2},{4,5},{5,4},{6,7},{7,6},{8,9},{9,8},{10,11... | collective-permute-start | bytes 67592 | tf_op jit(solution)/shard_map/ppermute | solution.py:62
  287.9 32.0 %collective-permute-start.30 = (bf16[704,1024]{1,0:T(8,128)(2,1)S(1)}, bf16[704,1024]{1,0:T(8,128)(2,1)S(1)}, u32[]{:S(2)}, u32[]{:S(2)}) collective-permute-start(bf16[704,1024]{1,0:T(8,128)(2,1)S(1)} %get-tuple-element.623), channel_id=1, source_target_pairs={{0,1},{1,0},{2,3},{3,2},{4,5},{5,4},{6,7},{7,6},{8,9},{9,8},{10,11... | collective-permute-start | bytes 4325384 | tf_op jit(solution)/shard_map/ppermute | solution.py:62
  288.9 31.7 %collective-permute-start.28 = (bf16[704,1024]{1,0:T(8,128)(2,1)S(1)}, bf16[704,1024]{1,0:T(8,128)(2,1)S(1)}, u32[]{:S(2)}, u32[]{:S(2)}) collective-permute-start(bf16[704,1024]{1,0:T(8,128)(2,1)S(1)} %get-tuple-element.619), channel_id=1, source_target_pairs={{0,4},{2,6},{4,0},{6,2},{1,5},{3,7},{5,1},{7,3},{8,12},{10,14},{12... | collective-permute-start | bytes 4325384 | tf_op jit(solution)/shard_map/ppermute | solution.py:61
  341.5 31.2 %collective-permute-start.36 = (bf16[352,2048]{1,0:T(8,128)(2,1)S(1)}, bf16[352,2048]{1,0:T(8,128)(2,1)S(1)}, u32[]{:S(2)}, u32[]{:S(2)}) collective-permute-start(bf16[352,2048]{1,0:T(8,128)(2,1)S(1)} %get-tuple-element.645), channel_id=1, source_target_pairs={{0,8},{24,16},{1,9},{25,17},{2,10},{26,18},{3,11},{27,19},{4,12},{... | collective-permute-start | bytes 4325384 | tf_op jit(solution)/shard_map/ppermute | solution.py:199
  347.1 29.7 %collective-permute-start.34 = (bf16[2,1,704,512]{3,2,1,0:T(8,128)(2,1)S(1)}, bf16[2,1,704,512]{3,2,1,0:T(8,128)(2,1)S(1)}, u32[]{:S(2)}, u32[]{:S(2)}) collective-permute-start(bf16[2,1,704,512]{3,2,1,0:T(8,128)(2,1)S(1)} %pad_maximum_fusion.4.own0_ref), channel_id=1, source_target_pairs={{0,1},{1,0},{2,3},{3,2},{4,5},{5,4},{6,7},{7,6},{8,9},{9,8},{10,11... | collective-permute-start | bytes 4325384 | tf_op jit(solution)/shard_map/ppermute | solution.py:62
  348.2 29.4 %collective-permute-start.35 = (bf16[1,2,704,512]{3,2,1,0:T(8,128)(2,1)S(1)}, bf16[1,2,704,512]{3,2,1,0:T(8,128)(2,1)S(1)}, u32[]{:S(2)}, u32[]{:S(2)}) collective-permute-start(bf16[1,2,704,512]{3,2,1,0:T(8,128)(2,1)S(1)} %pad_maximum_fusion.5.own1_ref), channel_id=1, source_target_pairs={{0,4},{2,6},{4,0},{6,2},{1,5},{3,7},{5,1},{7,3},{8,12},{10,14},{12... | collective-permute-start | bytes 4325384 | tf_op jit(solution)/shard_map/ppermute | solution.py:61
  349.7 31.5 %collective-permute-start.37 = (f32[2,1024]{1,0:T(2,128)S(1)}, f32[2,1024]{1,0:T(2,128)S(1)}, u32[]{:S(2)}, u32[]{:S(2)}) collective-permute-start(f32[2,1024]{1,0:T(2,128)S(1)} %add.401), channel_id=1, source_target_pairs={{0,4},{2,6},{4,0},{6,2},{1,5},{3,7},{5,1},{7,3},{8,12},{10,14},{12... | collective-permute-start | bytes 24584 | tf_op jit(solution)/shard_map/ppermute | solution.py:61
  384.0 28.9 %collective-permute-start.45 = (bf16[352,2048]{1,0:T(8,128)(2,1)S(1)}, bf16[352,2048]{1,0:T(8,128)(2,1)}, u32[]{:S(2)}, u32[]{:S(2)}) collective-permute-start(bf16[352,2048]{1,0:T(8,128)(2,1)S(1)} %reduce-precision_convert_fusion.11), channel_id=1, source_target_pairs={{8,16},{16,8},{9,17},{17,9},{10,18},{18,10},{11,19},{19,11},{12,20... | collective-permute-start | bytes 4325384 | tf_op jit(solution)/shard_map/ppermute | solution.py:205
  385.9 36.9 %collective-permute-start.44 = (bf16[352,2048]{1,0:T(8,128)(2,1)}, bf16[352,2048]{1,0:T(8,128)(2,1)}, u32[]{:S(2)}, u32[]{:S(2)}) collective-permute-start(bf16[352,2048]{1,0:T(8,128)(2,1)} %get-tuple-element.670), channel_id=1, source_target_pairs={{0,8},{24,16},{1,9},{25,17},{2,10},{26,18},{3,11},{27,19},{4,12},{... | collective-permute-start | bytes 4325384 | tf_op jit(solution)/shard_map/ppermute | solution.py:199
  398.3 33.5 %collective-permute-start.43 = (bf16[1,2,704,512]{3,2,1,0:T(8,128)(2,1)S(1)}, bf16[1,2,704,512]{3,2,1,0:T(8,128)(2,1)S(1)}, u32[]{:S(2)}, u32[]{:S(2)}) collective-permute-start(bf16[1,2,704,512]{3,2,1,0:T(8,128)(2,1)S(1)} %pad_maximum_fusion.7.own1_ref), channel_id=1, source_target_pairs={{0,4},{2,6},{4,0},{6,2},{1,5},{3,7},{5,1},{7,3},{8,12},{10,14},{12... | collective-permute-start | bytes 4325384 | tf_op jit(solution)/shard_map/ppermute | solution.py:61
  399.1 33.3 %collective-permute-start.42 = (bf16[2,1,704,512]{3,2,1,0:T(8,128)(2,1)S(1)}, bf16[2,1,704,512]{3,2,1,0:T(8,128)(2,1)}, u32[]{:S(2)}, u32[]{:S(2)}) collective-permute-start(bf16[2,1,704,512]{3,2,1,0:T(8,128)(2,1)S(1)} %pad_maximum_fusion.6.own0_ref), channel_id=1, source_target_pairs={{0,1},{1,0},{2,3},{3,2},{4,5},{5,4},{6,7},{7,6},{8,9},{9,8},{10,11... | collective-permute-start | bytes 4325384 | tf_op jit(solution)/shard_map/ppermute | solution.py:62
  443.1 38.8 %collective-permute-start.53 = (bf16[352,2048]{1,0:T(8,128)(2,1)}, bf16[352,2048]{1,0:T(8,128)(2,1)S(1)}, u32[]{:S(2)}, u32[]{:S(2)}) collective-permute-start(bf16[352,2048]{1,0:T(8,128)(2,1)} %reduce-precision_convert_fusion.10), channel_id=1, source_target_pairs={{8,16},{16,8},{9,17},{17,9},{10,18},{18,10},{11,19},{19,11},{12,20... | collective-permute-start | bytes 4325384 | tf_op jit(solution)/shard_map/ppermute | solution.py:205
  446.2 35.7 %collective-permute-start.52 = (bf16[352,2048]{1,0:T(8,128)(2,1)S(1)}, bf16[352,2048]{1,0:T(8,128)(2,1)S(1)}, u32[]{:S(2)}, u32[]{:S(2)}) collective-permute-start(bf16[352,2048]{1,0:T(8,128)(2,1)S(1)} %reduce-precision_convert_fusion.9), channel_id=1, source_target_pairs={{8,0},{16,24},{9,1},{17,25},{10,2},{18,26},{11,3},{19,27},{12,4},{... | collective-permute-start | bytes 4325384 | tf_op jit(solution)/shard_map/ppermute | solution.py:202
  447.5 35.7 %collective-permute-start.51 = (bf16[256,2816]{1,0:T(8,128)(2,1)S(1)}, bf16[256,2816]{1,0:T(8,128)(2,1)S(1)}, u32[]{:S(2)}, u32[]{:S(2)}) collective-permute-start(bf16[256,2816]{1,0:T(8,128)(2,1)S(1)} %copy-done.127), channel_id=1, source_target_pairs={{0,8},{24,16},{1,9},{25,17},{2,10},{26,18},{3,11},{27,19},{4,12},{... | collective-permute-start | bytes 4325384 | tf_op jit(solution)/shard_map/ppermute | solution.py:199
  462.6 33.7 %collective-permute-start.49 = (bf16[2,1,256,512]{3,2,1,0:T(8,128)(2,1)S(1)}, bf16[2,1,256,512]{3,2,1,0:T(8,128)(2,1)S(1)}, u32[]{:S(2)}, u32[]{:S(2)}) collective-permute-start(bf16[2,1,256,512]{3,2,1,0:T(8,128)(2,1)S(1)} %pad_maximum_fusion.14.own0_ref), channel_id=1, source_target_pairs={{0,1},{1,0},{2,3},{3,2},{4,5},{5,4},{6,7},{7,6},{8,9},{9,8},{10,11... | collective-permute-start | bytes 1572872 | tf_op jit(solution)/shard_map/ppermute | solution.py:62
  500.5 44.1 %collective-permute-start.59 = (bf16[256,2816]{1,0:T(8,128)(2,1)}, bf16[256,2816]{1,0:T(8,128)(2,1)}, u32[]{:S(2)}, u32[]{:S(2)}) collective-permute-start(bf16[256,2816]{1,0:T(8,128)(2,1)} %reduce-precision_convert_fusion.8), channel_id=1, source_target_pairs={{8,16},{16,8},{9,17},{17,9},{10,18},{18,10},{11,19},{19,11},{12,20... | collective-permute-start | bytes 4325384 | tf_op jit(solution)/shard_map/ppermute | solution.py:205
  505.5 39.1 %collective-permute-start.58 = (bf16[352,2048]{1,0:T(8,128)(2,1)}, bf16[352,2048]{1,0:T(8,128)(2,1)}, u32[]{:S(2)}, u32[]{:S(2)}) collective-permute-start(bf16[352,2048]{1,0:T(8,128)(2,1)} %reduce-precision_convert_fusion.7), channel_id=1, source_target_pairs={{8,0},{16,24},{9,1},{17,25},{10,2},{18,26},{11,3},{19,27},{12,4},{... | collective-permute-start | bytes 4325384 | tf_op jit(solution)/shard_map/ppermute | solution.py:202
  506.8 37.8 %collective-permute-start.57 = (bf16[256,2816]{1,0:T(8,128)(2,1)}, bf16[256,2816]{1,0:T(8,128)(2,1)}, u32[]{:S(2)}, u32[]{:S(2)}) collective-permute-start(bf16[256,2816]{1,0:T(8,128)(2,1)} %get-tuple-element.726), channel_id=1, source_target_pairs={{0,8},{24,16},{1,9},{25,17},{2,10},{26,18},{3,11},{27,19},{4,12},{... | collective-permute-start | bytes 4325384 | tf_op jit(solution)/shard_map/ppermute | solution.py:199
  546.9 33.5 %collective-permute-start.62 = (bf16[256,2816]{1,0:T(8,128)(2,1)S(1)}, bf16[256,2816]{1,0:T(8,128)(2,1)S(1)}, u32[]{:S(2)}, u32[]{:S(2)}) collective-permute-start(bf16[256,2816]{1,0:T(8,128)(2,1)S(1)} %fusion), channel_id=1, source_target_pairs={{0,8},{8,0},{16,24},{24,16},{1,9},{9,1},{17,25},{25,17},{2,10},{10... | collective-permute-start | bytes 4325384 | tf_op jit(solution)/shard_map/ppermute | solution.py:194
  551.4 29.0 %collective-permute-start.63 = (bf16[256,2816]{1,0:T(8,128)(2,1)S(1)}, bf16[256,2816]{1,0:T(8,128)(2,1)}, u32[]{:S(2)}, u32[]{:S(2)}) collective-permute-start(bf16[256,2816]{1,0:T(8,128)(2,1)S(1)} %reduce-precision_convert_fusion.6), channel_id=1, source_target_pairs={{8,16},{16,8},{9,17},{17,9},{10,18},{18,10},{11,19},{19,11},{12,20... | collective-permute-start | bytes 4325384 | tf_op jit(solution)/shard_map/ppermute | solution.py:205
  556.2 36.9 %collective-permute-start.60 = (bf16[2,1,768,512]{3,2,1,0:T(8,128)(2,1)S(1)}, bf16[2,1,768,512]{3,2,1,0:T(8,128)(2,1)S(1)}, u32[]{:S(2)}, u32[]{:S(2)}) collective-permute-start(bf16[2,1,768,512]{3,2,1,0:T(8,128)(2,1)S(1)} %pad_maximum_fusion.1.own0_ref), channel_id=1, source_target_pairs={{0,1},{1,0},{2,3},{3,2},{4,5},{5,4},{6,7},{7,6},{8,9},{9,8},{10,11... | collective-permute-start | bytes 4718600 | tf_op jit(solution)/shard_map/ppermute | solution.py:62
  557.5 35.6 %collective-permute-start.61 = (bf16[1,2,768,512]{3,2,1,0:T(8,128)(2,1)S(1)}, bf16[1,2,768,512]{3,2,1,0:T(8,128)(2,1)}, u32[]{:S(2)}, u32[]{:S(2)}) collective-permute-start(bf16[1,2,768,512]{3,2,1,0:T(8,128)(2,1)S(1)} %pad_maximum_fusion.2.own1_ref), channel_id=1, source_target_pairs={{0,4},{2,6},{4,0},{6,2},{1,5},{3,7},{5,1},{7,3},{8,12},{10,14},{12... | collective-permute-start | bytes 4718600 | tf_op jit(solution)/shard_map/ppermute | solution.py:61
  584.0 36.2 %collective-permute-start.64 = (bf16[256,2816]{1,0:T(8,128)(2,1)}, bf16[256,2816]{1,0:T(8,128)(2,1)S(1)}, u32[]{:S(2)}, u32[]{:S(2)}) collective-permute-start(bf16[256,2816]{1,0:T(8,128)(2,1)} %fusion.1), channel_id=1, source_target_pairs={{0,8},{8,0},{16,24},{24,16},{1,9},{9,1},{17,25},{25,17},{2,10},{10... | collective-permute-start | bytes 4325384 | tf_op jit(solution)/shard_map/ppermute | solution.py:194
  590.2 30.1 %collective-permute-start.65 = (bf16[256,2816]{1,0:T(8,128)(2,1)S(1)}, bf16[256,2816]{1,0:T(8,128)(2,1)S(1)}, u32[]{:S(2)}, u32[]{:S(2)}) collective-permute-start(bf16[256,2816]{1,0:T(8,128)(2,1)S(1)} %reduce-precision_convert_fusion.4), channel_id=1, source_target_pairs={{8,16},{16,8},{9,17},{17,9},{10,18},{18,10},{11,19},{19,11},{12,20... | collective-permute-start | bytes 4325384 | tf_op jit(solution)/shard_map/ppermute | solution.py:205
  635.3 37.5 %collective-permute-start.71 = (bf16[256,2816]{1,0:T(8,128)(2,1)}, bf16[256,2816]{1,0:T(8,128)(2,1)}, u32[]{:S(2)}, u32[]{:S(2)}) collective-permute-start(bf16[256,2816]{1,0:T(8,128)(2,1)} %reduce-precision_convert_fusion.1), channel_id=1, source_target_pairs={{8,0},{16,24},{9,1},{17,25},{10,2},{18,26},{11,3},{19,27},{12,4},{... | collective-permute-start | bytes 4325384 | tf_op jit(solution)/shard_map/ppermute | solution.py:202
  636.6 36.2 %collective-permute-start.72 = (bf16[256,2816]{1,0:T(8,128)(2,1)}, bf16[256,2816]{1,0:T(8,128)(2,1)}, u32[]{:S(2)}, u32[]{:S(2)}) collective-permute-start(bf16[256,2816]{1,0:T(8,128)(2,1)} %reduce-precision_convert_fusion.2), channel_id=1, source_target_pairs={{8,16},{16,8},{9,17},{17,9},{10,18},{18,10},{11,19},{19,11},{12,20... | collective-permute-start | bytes 4325384 | tf_op jit(solution)/shard_map/ppermute | solution.py:205
  638.4 31.5 %collective-permute-start.70 = (bf16[512,1024]{1,0:T(8,128)(2,1)}, bf16[512,1024]{1,0:T(8,128)(2,1)S(1)}, u32[]{:S(2)}, u32[]{:S(2)}) collective-permute-start(bf16[512,1024]{1,0:T(8,128)(2,1)} %pad_maximum_fusion.10), channel_id=1, source_target_pairs={{0,8},{24,16},{1,9},{25,17},{2,10},{26,18},{3,11},{27,19},{4,12},{... | collective-permute-start | bytes 3145736 | tf_op jit(solution)/shard_map/ppermute | solution.py:199
  649.7 42.8 %collective-permute-start.41 = (bf16[1024,1024]{1,0:T(8,128)(2,1)S(1)}, bf16[1024,1024]{1,0:T(8,128)(2,1)S(1)}, u32[]{:S(2)}, u32[]{:S(2)}) collective-permute-start(bf16[1024,1024]{1,0:T(8,128)(2,1)S(1)} %bitcast.205), channel_id=1, source_target_pairs={{0,2},{2,0},{4,6},{6,4},{1,3},{3,1},{5,7},{7,5},{8,10},{10,8},{12,... | collective-permute-start | bytes 6291464 | tf_op jit(solution)/shard_map/ppermute | solution.py:57
  676.0 37.9 %collective-permute-start.77 = (bf16[256,2816]{1,0:T(8,128)(2,1)}, bf16[256,2816]{1,0:T(8,128)(2,1)}, u32[]{:S(2)}, u32[]{:S(2)}) collective-permute-start(bf16[256,2816]{1,0:T(8,128)(2,1)} %reduce-precision_convert_fusion), channel_id=1, source_target_pairs={{8,0},{16,24},{9,1},{17,25},{10,2},{18,26},{11,3},{19,27},{12,4},{... | collective-permute-start | bytes 4325384 | tf_op jit(solution)/shard_map/ppermute | solution.py:202
  681.6 32.0 %collective-permute-start.76 = (bf16[512,1024]{1,0:T(8,128)(2,1)}, bf16[512,1024]{1,0:T(8,128)(2,1)}, u32[]{:S(2)}, u32[]{:S(2)}) collective-permute-start(bf16[512,1024]{1,0:T(8,128)(2,1)} %shard_map.347), channel_id=1, source_target_pairs={{0,8},{24,16},{1,9},{25,17},{2,10},{26,18},{3,11},{27,19},{4,12},{... | collective-permute-start | bytes 3145736 | tf_op jit(solution)/shard_map/ppermute | solution.py:199
  697.7 43.6 %collective-permute-start.73 = (bf16[512,1024]{1,0:T(8,128)(2,1)}, bf16[512,1024]{1,0:T(8,128)(2,1)}, u32[]{:S(2)}, u32[]{:S(2)}) collective-permute-start(bf16[512,1024]{1,0:T(8,128)(2,1)} %get-tuple-element.792), channel_id=1, source_target_pairs={{0,4},{2,6},{4,0},{6,2},{1,5},{3,7},{5,1},{7,3},{8,12},{10,14},{12... | collective-permute-start | bytes 3145736 | tf_op jit(solution)/shard_map/ppermute | solution.py:61
  724.0 39.0 %collective-permute-start.83 = (bf16[256,2816]{1,0:T(8,128)(2,1)}, bf16[256,2816]{1,0:T(8,128)(2,1)}, u32[]{:S(2)}, u32[]{:S(2)}) collective-permute-start(bf16[256,2816]{1,0:T(8,128)(2,1)} %broadcast_select_fusion), channel_id=1, source_target_pairs={{0,2},{2,0},{4,6},{6,4},{1,3},{3,1},{5,7},{7,5},{8,10},{10,8},{12,... | collective-permute-start | bytes 4325384 | tf_op jit(solution)/shard_map/ppermute | solution.py:57
  748.3 33.9 %collective-permute-start.84 = (bf16[512,1024]{1,0:T(8,128)(2,1)}, bf16[512,1024]{1,0:T(8,128)(2,1)}, u32[]{:S(2)}, u32[]{:S(2)}) collective-permute-start(bf16[512,1024]{1,0:T(8,128)(2,1)} %fusion.5), channel_id=1, source_target_pairs={{0,8},{8,0},{16,24},{24,16},{1,9},{9,1},{17,25},{25,17},{2,10},{10... | collective-permute-start | bytes 3145736 | tf_op jit(solution)/shard_map/ppermute | solution.py:194
  749.3 32.9 %collective-permute-start.85 = (bf16[512,1024]{1,0:T(8,128)(2,1)}, bf16[512,1024]{1,0:T(8,128)(2,1)}, u32[]{:S(2)}, u32[]{:S(2)}) collective-permute-start(bf16[512,1024]{1,0:T(8,128)(2,1)} %reduce-precision_convert_fusion.16), channel_id=1, source_target_pairs={{8,16},{16,8},{9,17},{17,9},{10,18},{18,10},{11,19},{19,11},{12,20... | collective-permute-start | bytes 3145736 | tf_op jit(solution)/shard_map/ppermute | solution.py:205
  784.3 27.4 %collective-permute-start.86 = (bf16[512,1024]{1,0:T(8,128)(2,1)S(1)}, bf16[512,1024]{1,0:T(8,128)(2,1)S(1)}, u32[]{:S(2)}, u32[]{:S(2)}) collective-permute-start(bf16[512,1024]{1,0:T(8,128)(2,1)S(1)} %reduce-precision_convert_fusion.13), channel_id=1, source_target_pairs={{8,0},{16,24},{9,1},{17,25},{10,2},{18,26},{11,3},{19,27},{12,4},{... | collective-permute-start | bytes 3145736 | tf_op jit(solution)/shard_map/ppermute | solution.py:202
  788.0 49.0 %collective-permute-start.79 = (bf16[256,1024]{1,0:T(8,128)(2,1)}, bf16[256,1024]{1,0:T(8,128)(2,1)}, u32[]{:S(2)}, u32[]{:S(2)}) collective-permute-start(bf16[256,1024]{1,0:T(8,128)(2,1)} %get-tuple-element.815), channel_id=1, source_target_pairs={{0,1},{1,0},{2,3},{3,2},{4,5},{5,4},{6,7},{7,6},{8,9},{9,8},{10,11... | collective-permute-start | bytes 1572872 | tf_op jit(solution)/shard_map/ppermute | solution.py:62
  791.2 45.9 %collective-permute-start.90 = (bf16[256,1024]{1,0:T(8,128)(2,1)}, bf16[256,1024]{1,0:T(8,128)(2,1)}, u32[]{:S(2)}, u32[]{:S(2)}) collective-permute-start(bf16[256,1024]{1,0:T(8,128)(2,1)} %get-tuple-element.973), channel_id=1, source_target_pairs={{0,2},{2,0},{4,6},{6,4},{1,3},{3,1},{5,7},{7,5},{8,10},{10,8},{12,... | collective-permute-start | bytes 1572872 | tf_op jit(solution)/shard_map/ppermute | solution.py:57
  813.1 37.3 %collective-permute-start.88 = (bf16[512,1024]{1,0:T(8,128)(2,1)}, bf16[512,1024]{1,0:T(8,128)(2,1)}, u32[]{:S(2)}, u32[]{:S(2)}) collective-permute-start(bf16[512,1024]{1,0:T(8,128)(2,1)} %reduce-precision_convert_fusion.12), channel_id=1, source_target_pairs={{8,0},{16,24},{9,1},{17,25},{10,2},{18,26},{11,3},{19,27},{12,4},{... | collective-permute-start | bytes 3145736 | tf_op jit(solution)/shard_map/ppermute | solution.py:202
  815.8 28.0 %collective-permute-start.89 = (bf16[256,1024]{1,0:T(8,128)(2,1)}, bf16[256,1024]{1,0:T(8,128)(2,1)}, u32[]{:S(2)}, u32[]{:S(2)}) collective-permute-start(bf16[256,1024]{1,0:T(8,128)(2,1)} %get-tuple-element.975), channel_id=1, source_target_pairs={{0,2},{2,0},{4,6},{6,4},{1,3},{3,1},{5,7},{7,5},{8,10},{10,8},{12,... | collective-permute-start | bytes 1572872 | tf_op jit(solution)/shard_map/ppermute | solution.py:57
  (210 other events, 1420.8 us)
where the time goes:
time: 891 us; the launch traced here: 880 us
  waiting for transfers between devices  247 us (28%)
  Pallas kernels  227 us (25%)
  starting transfers between devices  153 us (17%)
  local copies, waits for them, and re-layouts  109 us (12%)
  other arithmetic  89.6 us (10%)
  matrix products  38.1 us (4%)
  blocking collectives  11.8 us (1%)
    ppermute x21, waiting for transfers between devices, along(): return lax.ppermute(x, 'shard', [(i, i ^ step) for i in range(self.s_size)])  71.5 us
    pallas_call x9, Pallas kernels, adam_part(): pl.pallas_call(functools.partial(adam_kernel, rate, two), grid_spec=pltpu...  69.6 us
    unnamed x329, local copies, waits for them, and re-layouts  54.2 us
    ppermute x21, waiting for transfers between devices, along(): lax.ppermute(x, 'ctx', [(i, i ^ 2 * step) for i in range(self.ctx_size)])  50.8 us
    pallas_call x12, Pallas kernels, mm(): pl.pallas_call(functools.partial(product_kernel, dims), grid=(m // tm, n...  47.4 us
    ppermute x6, waiting for transfers between devices, tick(): slot['in_got'] = lax.ppermute(out['new'], 'rep', [(0, 1), (3, 2)])  42.6 us
    ppermute x6, waiting for transfers between devices, tick(): slot['out_got'] = lax.ppermute(out['total'], 'rep', [(1, 0), (2, 3)])  41.8 us
    ppermute x6, starting transfers between devices, tick(): slot['in_got'] = lax.ppermute(out['new'], 'rep', [(0, 1), (3, 2)])  41.6 us
  transfers between devices with their start and end apart: 95, of which 38 were waited for; matrix products, arithmetic and copies ran while one was open for 18% of the time, Pallas kernels for 22%

commit v1 on v0

--- a/solution.py
+++ b/solution.py
@@ -121,13 +121,11 @@
 
 class Order:
     def __init__(self):
-        self.last = None
+        self.token = lax.create_token()
 
     def __call__(self, stage, *args):
-        if self.last is not None:
-            args, self.last = lax.optimization_barrier((args, self.last))
-        out = stage(*args)
-        self.last = jax.tree.leaves(out)[0]
+        args, token = lax.optimization_barrier((args, self.token))
+        out, self.token = lax.optimization_barrier((stage(*args), token))
         return out
 
 

time: 891 us -> 855 us (0.960)
  waiting for transfers between devices: 247 us -> 264 us
  Pallas kernels: 227 us -> 213 us
  local copies, waits for them, and re-layouts: 109 us -> 96 us
  starting transfers between devices: 153 us -> 140 us
  blocking collectives: 11.8 us -> 0 us
    ppermute x21, waiting for transfers between devices: 71.5 us -> 113 us  [along(): return lax.ppermute(x, 'shard', [(i, i ^ step) for i in range(self.s_size)])]
    ppermute x21, waiting for transfers between devices: 50.8 us -> 30 us  [along(): lax.ppermute(x, 'ctx', [(i, i ^ 2 * step) for i in range(self.ctx_size)])]
    ppermute x4, waiting for transfers between devices: 25.2 us -> 10.7 us  [tick(): got = lax.ppermute(out['total'], 'rep', [(0, 1), (1, 0), (2, 3), (3, 2)])]
    ppermute x6, waiting for transfers between devices: 42.6 us -> 55.4 us  [tick(): slot['in_got'] = lax.ppermute(out['new'], 'rep', [(0, 1), (3, 2)])]
    all_to_all x1 -> x0, blocking collectives: 11.8 us -> none  [to_rows(): got = lax.all_to_all(split, plane, split_axis=0, concat_axis=0, tiled=True)]
    ppermute x6, waiting for transfers between devices: 41.8 us -> 30.2 us  [tick(): slot['out_got'] = lax.ppermute(out['total'], 'rep', [(1, 0), (2, 3)])]
    ppermute x2, starting transfers between devices: 15.9 us -> 4.81 us  [small_step(): lax.ppermute(small, 'rep', [(i, i ^ k) for i in range(lax.axis_size('rep'...]
    pallas_call x6, Pallas kernels: 17.2 us -> 7.3 us  [arrange(): pl.pallas_call(arrange_kernel, grid_spec=pltpu.PrefetchScalarGridSpec(num...]
  transfers between devices with their start and end apart: 95 -> 96, of which waited for: 38 -> 49; matrix products, arithmetic and copies ran while one was open for 18% -> 16% of each run, Pallas kernels for 22% -> 21%
where the time goes in v1:
time: 855 us; the launch traced here: 842 us
  waiting for transfers between devices  264 us (31%)
  Pallas kernels  213 us (25%)
  starting transfers between devices  140 us (16%)
  local copies, waits for them, and re-layouts  96 us (11%)
  other arithmetic  87.8 us (10%)
  matrix products  38 us (4%)
    ppermute x21, waiting for transfers between devices, along(): return lax.ppermute(x, 'shard', [(i, i ^ step) for i in range(self.s_size)])  113 us
    pallas_call x9, Pallas kernels, adam_part(): pl.pallas_call(functools.partial(adam_kernel, rate, two), grid_spec=pltpu...  69 us
    ppermute x6, waiting for transfers between devices, tick(): slot['in_got'] = lax.ppermute(out['new'], 'rep', [(0, 1), (3, 2)])  55.4 us
    unnamed x280, local copies, waits for them, and re-layouts  54.7 us
    pallas_call x12, Pallas kernels, mm(): pl.pallas_call(functools.partial(product_kernel, dims), grid=(m // tm, n...  47 us
    dot_general x18, matrix products, dot(): return lax.dot_general(a, b, dims, preferred_element_type=f32)  38 us
    convert_element_type x16, other arithmetic, add(): lax.reduce_precision(a.astype(f32) + b.astype(f32), 8, 7).astype(bf16)  33.6 us
    ppermute x6, starting transfers between devices, tick(): slot['in_got'] = lax.ppermute(out['new'], 'rep', [(0, 1), (3, 2)])  32 us
  transfers between devices with their start and end apart: 96, of which 49 were waited for; matrix products, arithmetic and copies ran while one was open for 16% of the time, Pallas kernels for 21%

profile of v1, /device:TPU:0, one launch (start us, length us, event | category | flops | bytes accessed | tf_op | source)
XLA Modules:
  0.0 841.8 jit_solution(11146650072471821606)
XLA Ops:
  12.9 4.8 all-to-all-start
  72.8 11.1 %collective-permute-done.5.b_ref.d_ref = bf16[1536,512]{1,0:T(8,128)(2,1)} collective-permute-done((bf16[1536,512]{1,0:T(8,128)(2,1)}, bf16[1536,512]{1,0:T(8,128)(2,1)}, u32[]{:S(2)}, u32[]{:S(2)}) %collective-permute-start.5) | collective-permute-done | bytes 1572896 | tf_op jit(solution)/shard_map/ppermute | solution.py:62
  101.9 10.8 %collective-permute-done.6 = bf16[768,512]{1,0:T(8,128)(2,1)S(1)} collective-permute-done((bf16[768,512]{1,0:T(8,128)(2,1)S(1)}, bf16[768,512]{1,0:T(8,128)(2,1)S(1)}, u32[]{:S(2)}, u32[]{:S(2)}) %collective-permute-start.6) | collective-permute-done | bytes 786464 | tf_op jit(solution)/shard_map/ppermute | solution.py:61
  126.1 4.5 shard_map.316
  151.0 8.8 %collective-permute-done.13.b_ref.d_ref = bf16[512,512]{1,0:T(8,128)(2,1)} collective-permute-done((bf16[512,512]{1,0:T(8,128)(2,1)}, bf16[512,512]{1,0:T(8,128)(2,1)}, u32[]{:S(2)}, u32[]{:S(2)}) %collective-permute-start.13) | collective-permute-done | bytes 524320 | tf_op jit(solution)/shard_map/ppermute | solution.py:62
  167.6 5.0 collective-permute-done.18
  200.1 5.0 convolution_convert_fusion.1.a_ref.c_ref
  218.5 5.1 shard_map.324.b_ref.x_ref
  225.7 5.5 shard_map.325.grad_ref
  240.7 13.7 %collective-permute-done.24 = f32[4,2,1,704]{3,0,2,1:T(4,128)S(1)} collective-permute-done((f32[4,2,1,704]{3,0,2,1:T(4,128)S(1)}, f32[4,2,1,704]{3,0,2,1:T(4,128)S(1)}, u32[]{:S(2)}, u32[]{:S(2)}) %collective-permute-start.24) | collective-permute-done | bytes 22560 | tf_op jit(solution)/shard_map/ppermute | solution.py:62
  257.7 8.2 collective-permute-done.27
  277.0 29.4 %collective-permute-done.30.ub_ref = bf16[704,1024]{1,0:T(8,128)(2,1)S(1)} collective-permute-done((bf16[704,1024]{1,0:T(8,128)(2,1)S(1)}, bf16[704,1024]{1,0:T(8,128)(2,1)S(1)}, u32[]{:S(2)}, u32[]{:S(2)}) %collective-permute-start.30) | collective-permute-done | bytes 1441824 | tf_op jit(solution)/shard_map/ppermute | solution.py:62
  308.6 7.5 shard_map.331
  320.1 5.4 shard_map.332
  338.0 21.3 %collective-permute-done.36 = bf16[352,2048]{1,0:T(8,128)(2,1)S(1)} collective-permute-done((bf16[352,2048]{1,0:T(8,128)(2,1)S(1)}, bf16[352,2048]{1,0:T(8,128)(2,1)S(1)}, u32[]{:S(2)}, u32[]{:S(2)}) %collective-permute-start.36) | collective-permute-done | bytes 1441824 | tf_op jit(solution)/shard_map/ppermute | solution.py:197
  370.8 4.8 collective-permute-start.44
  377.4 5.7 shard_map.334
  387.9 5.8 shard_map.335
  393.7 5.3 shard_map.336
  399.0 7.1 collective-permute-done.44
  411.5 5.9 collective-permute-done.42.got0_ref
  421.7 5.2 convolution_add_fusion.2
  436.5 5.9 shard_map.338
  442.8 17.6 %collective-permute-done.51 = bf16[256,2816]{1,0:T(8,128)(2,1)S(1)} collective-permute-done((bf16[256,2816]{1,0:T(8,128)(2,1)S(1)}, bf16[256,2816]{1,0:T(8,128)(2,1)S(1)}, u32[]{:S(2)}, u32[]{:S(2)}) %collective-permute-start.51) | collective-permute-done | bytes 1441824 | tf_op jit(solution)/shard_map/ppermute | solution.py:197
  471.4 6.4 collective-permute-done.49.got0_ref
  496.1 5.5 shard_map.340
  501.6 5.4 shard_map.341
  510.5 7.8 shard_map.344
  537.1 5.9 collective-permute-done.56
  544.7 8.2 shard_map.345
  555.4 9.7 %collective-permute-done.62 = bf16[256,2816]{1,0:T(8,128)(2,1)S(1)} collective-permute-done((bf16[256,2816]{1,0:T(8,128)(2,1)S(1)}, bf16[256,2816]{1,0:T(8,128)(2,1)S(1)}, u32[]{:S(2)}, u32[]{:S(2)}) %collective-permute-start.62) | collective-permute-done | bytes 1441824 | tf_op jit(solution)/shard_map/ppermute | solution.py:192
  574.0 13.7 %collective-permute-done.60.got0_ref = bf16[2,1,768,512]{3,2,1,0:T(8,128)(2,1)S(1)} collective-permute-done((bf16[2,1,768,512]{3,2,1,0:T(8,128)(2,1)S(1)}, bf16[2,1,768,512]{3,2,1,0:T(8,128)(2,1)S(1)}, u32[]{:S(2)}, u32[]{:S(2)}) %collective-permute-start.60) | collective-permute-done | bytes 1572896 | tf_op jit(solution)/shard_map/ppermute | solution.py:62
  589.6 9.2 %shard_map.346 = bf16[3,2,2,256,1024]{4,3,2,1,0:T(8,128)(2,1)} custom-call(s32[4]{0:T(128)S(1)} %pad_add_fusion.1.bits_ref, bf16[2,1,768,512]{3,2,1,0:T(8,128)(2,1)S(1)} %pad_maximum_fusion.1.own0_ref, bf16[2,1,768,512]{3,2,1,0:T(8,128)(2,1)S(1)} %collective-permute-done.60.got0_ref, bf16[1,2,768,512]{3,2,1,0:T(8,128)(2,1)S(1)} %pad_maximum_fusion.2.own1_ref, ...), custom_call_target="tpu_custom_call" | custom-call | flops 1024 | bytes 1024 | tf_op jit(solution)/shard_map/pallas_call | solution.py:409
  614.0 5.9 shard_map.350
  623.6 8.4 collective-permute-start.70
  646.3 7.6 collective-permute-done.70
  664.4 8.7 %collective-permute-start.76 = (bf16[512,1024]{1,0:T(8,128)(2,1)}, bf16[512,1024]{1,0:T(8,128)(2,1)}, u32[]{:S(2)}, u32[]{:S(2)}) collective-permute-start(bf16[512,1024]{1,0:T(8,128)(2,1)} %shard_map.347), channel_id=1, source_target_pairs={{0,8},{24,16},{1,9},{25,17},{2,10},{26,18},{3,11},{27,19},{4,12},{... | collective-permute-start | bytes 3145736 | tf_op jit(solution)/shard_map/ppermute | solution.py:197
  687.4 6.2 all-to-all-done.1
  709.1 13.2 %shard_map.352 = (f32[256,11264]{1,0:T(8,128)}, f32[256,11264]{1,0:T(8,128)}, f32[256,11264]{1,0:T(8,128)}) custom-call(s32[1]{0:T(128)} %bitcast.8.core_ref, f32[256,11264]{1,0:T(8,128)} %w_ref.9, f32[256,11264]{1,0:T(8,128)} %m_ref.3, f32[256,11264]{1,0:T(8,128)} %v_ref.3, bf16[256,2816]{1,0:T(8,128)(2,1)S(1)} %broadcast_select_fusion.3.refs_0_, ...), custom_call_target="tpu_custom_call" | custom-call | flops 1024 | bytes 1024 | tf_op jit(solution)/shard_map/pallas_call | solution.py:520
  722.3 4.5 collective-permute-start.82
  746.3 5.7 all-to-all-done.2
  753.7 14.4 %shard_map.354 = (f32[256,11264]{1,0:T(8,128)}, f32[256,11264]{1,0:T(8,128)}, f32[256,11264]{1,0:T(8,128)}) custom-call(s32[1]{0:T(128)} %bitcast.8.core_ref, f32[256,11264]{1,0:T(8,128)} %w_ref.9, f32[256,11264]{1,0:T(8,128)} %m_ref.3, f32[256,11264]{1,0:T(8,128)} %v_ref.3, ...), custom_call_target="tpu_custom_call", output_to_operand_aliasing={{0}: (6, {}), {1}: (7, {}), {2}: (8, {})} | custom-call | flops 1024 | bytes 1024 | tf_op jit(solution)/shard_map/pallas_call | solution.py:520
  791.3 6.5 all-to-all-done.3
  798.8 4.5 collective-permute-done.86
  807.7 6.2 shard_map.357
  814.0 6.2 shard_map.358
  820.2 13.0 %collective-permute-done.88 = bf16[512,1024]{1,0:T(8,128)(2,1)S(1)} collective-permute-done((bf16[512,1024]{1,0:T(8,128)(2,1)S(1)}, bf16[512,1024]{1,0:T(8,128)(2,1)S(1)}, u32[]{:S(2)}, u32[]{:S(2)}) %collective-permute-start.88) | collective-permute-done | bytes 1048608 | tf_op jit(solution)/shard_map/ppermute | solution.py:200
  835.3 6.2 shard_map.359
  (675 shorter events, 440.2 us)
Async XLA Ops:
  46.2 37.7 %collective-permute-start.5 = (bf16[1536,512]{1,0:T(8,128)(2,1)}, bf16[1536,512]{1,0:T(8,128)(2,1)}, u32[]{:S(2)}, u32[]{:S(2)}) collective-permute-start(bf16[1536,512]{1,0:T(8,128)(2,1)} %convolution_convert_fusion.7), channel_id=1, source_target_pairs={{0,1},{1,0},{2,3},{3,2},{4,5},{5,4},{6,7},{7,6},{8,9},{9,8},{10,11... | collective-permute-start | bytes 4718600 | tf_op jit(solution)/shard_map/ppermute | solution.py:62
  47.5 40.4 %collective-permute-start.9 = (bf16[1536,512]{1,0:T(8,128)(2,1)}, bf16[1536,512]{1,0:T(8,128)(2,1)}, u32[]{:S(2)}, u32[]{:S(2)}) collective-permute-start(bf16[1536,512]{1,0:T(8,128)(2,1)} %convolution_convert_fusion.6), channel_id=1, source_target_pairs={{0,4},{2,6},{4,0},{6,2},{1,5},{3,7},{5,1},{7,3},{8,12},{10,14},{12... | collective-permute-start | bytes 4718600 | tf_op jit(solution)/shard_map/ppermute | solution.py:61
  63.7 30.3 %collective-permute-start.7 = (bf16[2,1,64,2048]{3,2,1,0:T(8,128)(2,1)}, bf16[2,1,64,2048]{3,2,1,0:T(8,128)(2,1)}, u32[]{:S(2)}, u32[]{:S(2)}) collective-permute-start(bf16[2,1,64,2048]{3,2,1,0:T(8,128)(2,1)} %pad_maximum_fusion.12), channel_id=1, source_target_pairs={{0,1},{1,0},{2,3},{3,2},{4,5},{5,4},{6,7},{7,6},{8,9},{9,8},{10,11... | collective-permute-start | bytes 1572872 | tf_op jit(solution)/shard_map/ppermute | solution.py:62
  64.6 30.1 %collective-permute-start.8 = (bf16[1,2,64,2048]{3,2,1,0:T(8,128)(2,1)}, bf16[1,2,64,2048]{3,2,1,0:T(8,128)(2,1)}, u32[]{:S(2)}, u32[]{:S(2)}) collective-permute-start(bf16[1,2,64,2048]{3,2,1,0:T(8,128)(2,1)} %pad_maximum_fusion.13), channel_id=1, source_target_pairs={{0,4},{2,6},{4,0},{6,2},{1,5},{3,7},{5,1},{7,3},{8,12},{10,14},{12... | collective-permute-start | bytes 1572872 | tf_op jit(solution)/shard_map/ppermute | solution.py:61
  96.3 27.0 %collective-permute-start.11 = (bf16[768,512]{1,0:T(8,128)(2,1)}, bf16[768,512]{1,0:T(8,128)(2,1)}, u32[]{:S(2)}, u32[]{:S(2)}) collective-permute-start(bf16[768,512]{1,0:T(8,128)(2,1)} %get-tuple-element.1051), channel_id=1, source_target_pairs={{0,1},{1,0},{2,3},{3,2},{4,5},{5,4},{6,7},{7,6},{8,9},{9,8},{10,11... | collective-permute-start | bytes 2359304 | tf_op jit(solution)/shard_map/ppermute | solution.py:62
  189.1 77.6 %collective-permute-start.23 = (bf16[1408,1024]{1,0:T(8,128)(2,1)}, bf16[1408,1024]{1,0:T(8,128)(2,1)}, u32[]{:S(2)}, u32[]{:S(2)}) collective-permute-start(bf16[1408,1024]{1,0:T(8,128)(2,1)} %convolution_convert_fusion.3), channel_id=1, source_target_pairs={{0,1},{1,0},{2,3},{3,2},{4,5},{5,4},{6,7},{7,6},{8,9},{9,8},{10,11... | collective-permute-start | bytes 8650760 | tf_op jit(solution)/shard_map/ppermute | solution.py:62
  193.2 76.5 %collective-permute-start.29 = (bf16[1408,1024]{1,0:T(8,128)(2,1)}, bf16[1408,1024]{1,0:T(8,128)(2,1)}, u32[]{:S(2)}, u32[]{:S(2)}) collective-permute-start(bf16[1408,1024]{1,0:T(8,128)(2,1)} %convolution_convert_fusion.2), channel_id=1, source_target_pairs={{0,4},{2,6},{4,0},{6,2},{1,5},{3,7},{5,1},{7,3},{8,12},{10,14},{12... | collective-permute-start | bytes 8650760 | tf_op jit(solution)/shard_map/ppermute | solution.py:61
  195.0 23.6 %collective-permute-start.26 = (bf16[2,2,64,2048]{3,2,1,0:T(8,128)(2,1)}, bf16[2,2,64,2048]{3,2,1,0:T(8,128)(2,1)}, u32[]{:S(2)}, u32[]{:S(2)}) collective-permute-start(bf16[2,2,64,2048]{3,2,1,0:T(8,128)(2,1)} %pad_maximum_fusion.8.b_ref), channel_id=1, source_target_pairs={{0,2},{2,0},{4,6},{6,4},{1,3},{3,1},{5,7},{7,5},{8,10},{10,8},{12,... | collective-permute-start | bytes 3145736 | tf_op jit(solution)/shard_map/ppermute | solution.py:57
  197.1 57.3 %collective-permute-start.24 = (f32[4,2,1,704]{3,0,2,1:T(4,128)S(1)}, f32[4,2,1,704]{3,0,2,1:T(4,128)S(1)}, u32[]{:S(2)}, u32[]{:S(2)}) collective-permute-start(f32[4,2,1,704]{3,0,2,1:T(4,128)S(1)} %constant_dynamic-slice_fusion.4), channel_id=1, source_target_pairs={{0,1},{1,0},{2,3},{3,2},{4,5},{5,4},{6,7},{7,6},{8,9},{9,8},{10,11... | collective-permute-start | bytes 67592 | tf_op jit(solution)/shard_map/ppermute | solution.py:62
  274.4 32.0 %collective-permute-start.30 = (bf16[704,1024]{1,0:T(8,128)(2,1)S(1)}, bf16[704,1024]{1,0:T(8,128)(2,1)S(1)}, u32[]{:S(2)}, u32[]{:S(2)}) collective-permute-start(bf16[704,1024]{1,0:T(8,128)(2,1)S(1)} %get-tuple-element.1255), channel_id=1, source_target_pairs={{0,1},{1,0},{2,3},{3,2},{4,5},{5,4},{6,7},{7,6},{8,9},{9,8},{10,11... | collective-permute-start | bytes 4325384 | tf_op jit(solution)/shard_map/ppermute | solution.py:62
  275.2 31.7 %collective-permute-start.28 = (bf16[704,1024]{1,0:T(8,128)(2,1)S(1)}, bf16[704,1024]{1,0:T(8,128)(2,1)S(1)}, u32[]{:S(2)}, u32[]{:S(2)}) collective-permute-start(bf16[704,1024]{1,0:T(8,128)(2,1)S(1)} %get-tuple-element.1245), channel_id=1, source_target_pairs={{0,4},{2,6},{4,0},{6,2},{1,5},{3,7},{5,1},{7,3},{8,12},{10,14},{12... | collective-permute-start | bytes 4325384 | tf_op jit(solution)/shard_map/ppermute | solution.py:61
  327.9 31.4 %collective-permute-start.36 = (bf16[352,2048]{1,0:T(8,128)(2,1)S(1)}, bf16[352,2048]{1,0:T(8,128)(2,1)S(1)}, u32[]{:S(2)}, u32[]{:S(2)}) collective-permute-start(bf16[352,2048]{1,0:T(8,128)(2,1)S(1)} %get-tuple-element.1300), channel_id=1, source_target_pairs={{0,8},{24,16},{1,9},{25,17},{2,10},{26,18},{3,11},{27,19},{4,12},{... | collective-permute-start | bytes 4325384 | tf_op jit(solution)/shard_map/ppermute | solution.py:197
  334.8 29.9 %collective-permute-start.34 = (bf16[2,1,704,512]{3,2,1,0:T(8,128)(2,1)S(1)}, bf16[2,1,704,512]{3,2,1,0:T(8,128)(2,1)S(1)}, u32[]{:S(2)}, u32[]{:S(2)}) collective-permute-start(bf16[2,1,704,512]{3,2,1,0:T(8,128)(2,1)S(1)} %pad_maximum_fusion.3.own0_ref), channel_id=1, source_target_pairs={{0,1},{1,0},{2,3},{3,2},{4,5},{5,4},{6,7},{7,6},{8,9},{9,8},{10,11... | collective-permute-start | bytes 4325384 | tf_op jit(solution)/shard_map/ppermute | solution.py:62
  335.9 29.6 %collective-permute-start.35 = (bf16[1,2,704,512]{3,2,1,0:T(8,128)(2,1)S(1)}, bf16[1,2,704,512]{3,2,1,0:T(8,128)(2,1)S(1)}, u32[]{:S(2)}, u32[]{:S(2)}) collective-permute-start(bf16[1,2,704,512]{3,2,1,0:T(8,128)(2,1)S(1)} %pad_maximum_fusion.4.own1_ref), channel_id=1, source_target_pairs={{0,4},{2,6},{4,0},{6,2},{1,5},{3,7},{5,1},{7,3},{8,12},{10,14},{12... | collective-permute-start | bytes 4325384 | tf_op jit(solution)/shard_map/ppermute | solution.py:61
  336.4 32.8 %collective-permute-start.37 = (f32[2,1024]{1,0:T(2,128)S(1)}, f32[2,1024]{1,0:T(2,128)S(1)}, u32[]{:S(2)}, u32[]{:S(2)}) collective-permute-start(f32[2,1024]{1,0:T(2,128)S(1)} %add.401), channel_id=1, source_target_pairs={{0,4},{2,6},{4,0},{6,2},{1,5},{3,7},{5,1},{7,3},{8,12},{10,14},{12... | collective-permute-start | bytes 24584 | tf_op jit(solution)/shard_map/ppermute | solution.py:61
  370.8 35.4 %collective-permute-start.44 = (bf16[352,2048]{1,0:T(8,128)(2,1)}, bf16[352,2048]{1,0:T(8,128)(2,1)}, u32[]{:S(2)}, u32[]{:S(2)}) collective-permute-start(bf16[352,2048]{1,0:T(8,128)(2,1)} %get-tuple-element.1350), channel_id=1, source_target_pairs={{0,8},{24,16},{1,9},{25,17},{2,10},{26,18},{3,11},{27,19},{4,12},{... | collective-permute-start | bytes 4325384 | tf_op jit(solution)/shard_map/ppermute | solution.py:197
  375.5 30.6 %collective-permute-start.45 = (bf16[352,2048]{1,0:T(8,128)(2,1)}, bf16[352,2048]{1,0:T(8,128)(2,1)}, u32[]{:S(2)}, u32[]{:S(2)}) collective-permute-start(bf16[352,2048]{1,0:T(8,128)(2,1)} %reduce-precision_convert_fusion.11), channel_id=1, source_target_pairs={{8,16},{16,8},{9,17},{17,9},{10,18},{18,10},{11,19},{19,11},{12,20... | collective-permute-start | bytes 4325384 | tf_op jit(solution)/shard_map/ppermute | solution.py:203
  383.6 33.8 %collective-permute-start.42 = (bf16[2,1,704,512]{3,2,1,0:T(8,128)(2,1)S(1)}, bf16[2,1,704,512]{3,2,1,0:T(8,128)(2,1)S(1)}, u32[]{:S(2)}, u32[]{:S(2)}) collective-permute-start(bf16[2,1,704,512]{3,2,1,0:T(8,128)(2,1)S(1)} %pad_maximum_fusion.5.own0_ref), channel_id=1, source_target_pairs={{0,1},{1,0},{2,3},{3,2},{4,5},{5,4},{6,7},{7,6},{8,9},{9,8},{10,11... | collective-permute-start | bytes 4325384 | tf_op jit(solution)/shard_map/ppermute | solution.py:62
  384.7 33.4 %collective-permute-start.43 = (bf16[1,2,704,512]{3,2,1,0:T(8,128)(2,1)S(1)}, bf16[1,2,704,512]{3,2,1,0:T(8,128)(2,1)S(1)}, u32[]{:S(2)}, u32[]{:S(2)}) collective-permute-start(bf16[1,2,704,512]{3,2,1,0:T(8,128)(2,1)S(1)} %pad_maximum_fusion.6.own1_ref), channel_id=1, source_target_pairs={{0,4},{2,6},{4,0},{6,2},{1,5},{3,7},{5,1},{7,3},{8,12},{10,14},{12... | collective-permute-start | bytes 4325384 | tf_op jit(solution)/shard_map/ppermute | solution.py:61
  428.2 32.2 %collective-permute-start.51 = (bf16[256,2816]{1,0:T(8,128)(2,1)S(1)}, bf16[256,2816]{1,0:T(8,128)(2,1)S(1)}, u32[]{:S(2)}, u32[]{:S(2)}) collective-permute-start(bf16[256,2816]{1,0:T(8,128)(2,1)S(1)} %copy-done.112), channel_id=1, source_target_pairs={{0,8},{24,16},{1,9},{25,17},{2,10},{26,18},{3,11},{27,19},{4,12},{... | collective-permute-start | bytes 4325384 | tf_op jit(solution)/shard_map/ppermute | solution.py:197
  430.1 34.5 %collective-permute-start.52 = (bf16[352,2048]{1,0:T(8,128)(2,1)S(1)}, bf16[352,2048]{1,0:T(8,128)(2,1)S(1)}, u32[]{:S(2)}, u32[]{:S(2)}) collective-permute-start(bf16[352,2048]{1,0:T(8,128)(2,1)S(1)} %reduce-precision_convert_fusion.9), channel_id=1, source_target_pairs={{8,0},{16,24},{9,1},{17,25},{10,2},{18,26},{11,3},{19,27},{12,4},{... | collective-permute-start | bytes 4325384 | tf_op jit(solution)/shard_map/ppermute | solution.py:200
  431.4 33.3 %collective-permute-start.53 = (bf16[352,2048]{1,0:T(8,128)(2,1)S(1)}, bf16[352,2048]{1,0:T(8,128)(2,1)S(1)}, u32[]{:S(2)}, u32[]{:S(2)}) collective-permute-start(bf16[352,2048]{1,0:T(8,128)(2,1)S(1)} %reduce-precision_convert_fusion.10), channel_id=1, source_target_pairs={{8,16},{16,8},{9,17},{17,9},{10,18},{18,10},{11,19},{19,11},{12,20... | collective-permute-start | bytes 4325384 | tf_op jit(solution)/shard_map/ppermute | solution.py:203
  483.8 36.2 %collective-permute-start.57 = (bf16[256,2816]{1,0:T(8,128)(2,1)}, bf16[256,2816]{1,0:T(8,128)(2,1)S(1)}, u32[]{:S(2)}, u32[]{:S(2)}) collective-permute-start(bf16[256,2816]{1,0:T(8,128)(2,1)} %get-tuple-element.1464), channel_id=1, source_target_pairs={{0,8},{24,16},{1,9},{25,17},{2,10},{26,18},{3,11},{27,19},{4,12},{... | collective-permute-start | bytes 4325384 | tf_op jit(solution)/shard_map/ppermute | solution.py:197
  488.3 35.8 %collective-permute-start.58 = (bf16[352,2048]{1,0:T(8,128)(2,1)}, bf16[352,2048]{1,0:T(8,128)(2,1)S(1)}, u32[]{:S(2)}, u32[]{:S(2)}) collective-permute-start(bf16[352,2048]{1,0:T(8,128)(2,1)} %reduce-precision_convert_fusion.7), channel_id=1, source_target_pairs={{8,0},{16,24},{9,1},{17,25},{10,2},{18,26},{11,3},{19,27},{12,4},{... | collective-permute-start | bytes 4325384 | tf_op jit(solution)/shard_map/ppermute | solution.py:200
  489.6 34.5 %collective-permute-start.59 = (bf16[256,2816]{1,0:T(8,128)(2,1)}, bf16[256,2816]{1,0:T(8,128)(2,1)S(1)}, u32[]{:S(2)}, u32[]{:S(2)}) collective-permute-start(bf16[256,2816]{1,0:T(8,128)(2,1)} %reduce-precision_convert_fusion.8), channel_id=1, source_target_pairs={{8,16},{16,8},{9,17},{17,9},{10,18},{18,10},{11,19},{19,11},{12,20... | collective-permute-start | bytes 4325384 | tf_op jit(solution)/shard_map/ppermute | solution.py:203
  531.1 34.0 %collective-permute-start.62 = (bf16[256,2816]{1,0:T(8,128)(2,1)S(1)}, bf16[256,2816]{1,0:T(8,128)(2,1)S(1)}, u32[]{:S(2)}, u32[]{:S(2)}) collective-permute-start(bf16[256,2816]{1,0:T(8,128)(2,1)S(1)} %fusion), channel_id=1, source_target_pairs={{0,8},{8,0},{16,24},{24,16},{1,9},{9,1},{17,25},{25,17},{2,10},{10... | collective-permute-start | bytes 4325384 | tf_op jit(solution)/shard_map/ppermute | solution.py:192
  534.8 30.3 %collective-permute-start.63 = (bf16[256,2816]{1,0:T(8,128)(2,1)S(1)}, bf16[256,2816]{1,0:T(8,128)(2,1)}, u32[]{:S(2)}, u32[]{:S(2)}) collective-permute-start(bf16[256,2816]{1,0:T(8,128)(2,1)S(1)} %reduce-precision_convert_fusion.6), channel_id=1, source_target_pairs={{8,16},{16,8},{9,17},{17,9},{10,18},{18,10},{11,19},{19,11},{12,20... | collective-permute-start | bytes 4325384 | tf_op jit(solution)/shard_map/ppermute | solution.py:203
  552.9 34.8 %collective-permute-start.60 = (bf16[2,1,768,512]{3,2,1,0:T(8,128)(2,1)S(1)}, bf16[2,1,768,512]{3,2,1,0:T(8,128)(2,1)S(1)}, u32[]{:S(2)}, u32[]{:S(2)}) collective-permute-start(bf16[2,1,768,512]{3,2,1,0:T(8,128)(2,1)S(1)} %pad_maximum_fusion.1.own0_ref), channel_id=1, source_target_pairs={{0,1},{1,0},{2,3},{3,2},{4,5},{5,4},{6,7},{7,6},{8,9},{9,8},{10,11... | collective-permute-start | bytes 4718600 | tf_op jit(solution)/shard_map/ppermute | solution.py:62
  553.9 34.5 %collective-permute-start.61 = (bf16[1,2,768,512]{3,2,1,0:T(8,128)(2,1)S(1)}, bf16[1,2,768,512]{3,2,1,0:T(8,128)(2,1)S(1)}, u32[]{:S(2)}, u32[]{:S(2)}) collective-permute-start(bf16[1,2,768,512]{3,2,1,0:T(8,128)(2,1)S(1)} %pad_maximum_fusion.2.own1_ref), channel_id=1, source_target_pairs={{0,4},{2,6},{4,0},{6,2},{1,5},{3,7},{5,1},{7,3},{8,12},{10,14},{12... | collective-permute-start | bytes 4718600 | tf_op jit(solution)/shard_map/ppermute | solution.py:61
  569.0 35.8 %collective-permute-start.64 = (bf16[256,2816]{1,0:T(8,128)(2,1)S(1)}, bf16[256,2816]{1,0:T(8,128)(2,1)S(1)}, u32[]{:S(2)}, u32[]{:S(2)}) collective-permute-start(bf16[256,2816]{1,0:T(8,128)(2,1)S(1)} %fusion.1), channel_id=1, source_target_pairs={{0,8},{8,0},{16,24},{24,16},{1,9},{9,1},{17,25},{25,17},{2,10},{10... | collective-permute-start | bytes 4325384 | tf_op jit(solution)/shard_map/ppermute | solution.py:192
  572.2 32.5 %collective-permute-start.65 = (bf16[256,2816]{1,0:T(8,128)(2,1)S(1)}, bf16[256,2816]{1,0:T(8,128)(2,1)}, u32[]{:S(2)}, u32[]{:S(2)}) collective-permute-start(bf16[256,2816]{1,0:T(8,128)(2,1)S(1)} %reduce-precision_convert_fusion.4), channel_id=1, source_target_pairs={{8,16},{16,8},{9,17},{17,9},{10,18},{18,10},{11,19},{19,11},{12,20... | collective-permute-start | bytes 4325384 | tf_op jit(solution)/shard_map/ppermute | solution.py:203
  620.4 36.4 %collective-permute-start.71 = (bf16[256,2816]{1,0:T(8,128)(2,1)}, bf16[256,2816]{1,0:T(8,128)(2,1)}, u32[]{:S(2)}, u32[]{:S(2)}) collective-permute-start(bf16[256,2816]{1,0:T(8,128)(2,1)} %reduce-precision_convert_fusion.1), channel_id=1, source_target_pairs={{8,0},{16,24},{9,1},{17,25},{10,2},{18,26},{11,3},{19,27},{12,4},{... | collective-permute-start | bytes 4325384 | tf_op jit(solution)/shard_map/ppermute | solution.py:200
  621.8 35.0 %collective-permute-start.72 = (bf16[256,2816]{1,0:T(8,128)(2,1)}, bf16[256,2816]{1,0:T(8,128)(2,1)}, u32[]{:S(2)}, u32[]{:S(2)}) collective-permute-start(bf16[256,2816]{1,0:T(8,128)(2,1)} %reduce-precision_convert_fusion.2), channel_id=1, source_target_pairs={{8,16},{16,8},{9,17},{17,9},{10,18},{18,10},{11,19},{19,11},{12,20... | collective-permute-start | bytes 4325384 | tf_op jit(solution)/shard_map/ppermute | solution.py:203
  623.6 30.3 %collective-permute-start.70 = (bf16[512,1024]{1,0:T(8,128)(2,1)}, bf16[512,1024]{1,0:T(8,128)(2,1)}, u32[]{:S(2)}, u32[]{:S(2)}) collective-permute-start(bf16[512,1024]{1,0:T(8,128)(2,1)} %pad_maximum_fusion.10), channel_id=1, source_target_pairs={{0,8},{24,16},{1,9},{25,17},{2,10},{26,18},{3,11},{27,19},{4,12},{... | collective-permute-start | bytes 3145736 | tf_op jit(solution)/shard_map/ppermute | solution.py:197
  645.8 49.8 %collective-permute-start.41 = (bf16[1024,1024]{1,0:T(8,128)(2,1)}, bf16[1024,1024]{1,0:T(8,128)(2,1)}, u32[]{:S(2)}, u32[]{:S(2)}) collective-permute-start(bf16[1024,1024]{1,0:T(8,128)(2,1)} %bitcast.55), channel_id=1, source_target_pairs={{0,2},{2,0},{4,6},{6,4},{1,3},{3,1},{5,7},{7,5},{8,10},{10,8},{12,... | collective-permute-start | bytes 6291464 | tf_op jit(solution)/shard_map/ppermute | solution.py:57
  663.1 37.7 %collective-permute-start.77 = (bf16[256,2816]{1,0:T(8,128)(2,1)}, bf16[256,2816]{1,0:T(8,128)(2,1)}, u32[]{:S(2)}, u32[]{:S(2)}) collective-permute-start(bf16[256,2816]{1,0:T(8,128)(2,1)} %reduce-precision_convert_fusion), channel_id=1, source_target_pairs={{8,0},{16,24},{9,1},{17,25},{10,2},{18,26},{11,3},{19,27},{12,4},{... | collective-permute-start | bytes 4325384 | tf_op jit(solution)/shard_map/ppermute | solution.py:200
  664.4 34.2 %collective-permute-start.76 = (bf16[512,1024]{1,0:T(8,128)(2,1)}, bf16[512,1024]{1,0:T(8,128)(2,1)}, u32[]{:S(2)}, u32[]{:S(2)}) collective-permute-start(bf16[512,1024]{1,0:T(8,128)(2,1)} %shard_map.347), channel_id=1, source_target_pairs={{0,8},{24,16},{1,9},{25,17},{2,10},{26,18},{3,11},{27,19},{4,12},{... | collective-permute-start | bytes 3145736 | tf_op jit(solution)/shard_map/ppermute | solution.py:197
  673.1 26.1 %collective-permute-start.78 = (bf16[512,1024]{1,0:T(8,128)(2,1)}, bf16[512,1024]{1,0:T(8,128)(2,1)}, u32[]{:S(2)}, u32[]{:S(2)}) collective-permute-start(bf16[512,1024]{1,0:T(8,128)(2,1)} %reduce-precision_convert_fusion.19), channel_id=1, source_target_pairs={{8,16},{16,8},{9,17},{17,9},{10,18},{18,10},{11,19},{19,11},{12,20... | collective-permute-start | bytes 3145736 | tf_op jit(solution)/shard_map/ppermute | solution.py:203
  698.6 28.2 %collective-permute-start.73 = (bf16[512,1024]{1,0:T(8,128)(2,1)S(1)}, bf16[512,1024]{1,0:T(8,128)(2,1)S(1)}, u32[]{:S(2)}, u32[]{:S(2)}) collective-permute-start(bf16[512,1024]{1,0:T(8,128)(2,1)S(1)} %get-tuple-element.1604), channel_id=1, source_target_pairs={{0,4},{2,6},{4,0},{6,2},{1,5},{3,7},{5,1},{7,3},{8,12},{10,14},{12... | collective-permute-start | bytes 3145736 | tf_op jit(solution)/shard_map/ppermute | solution.py:61
  705.3 24.0 %collective-permute-start.80 = (bf16[512,1024]{1,0:T(8,128)(2,1)S(1)}, bf16[512,1024]{1,0:T(8,128)(2,1)S(1)}, u32[]{:S(2)}, u32[]{:S(2)}) collective-permute-start(bf16[512,1024]{1,0:T(8,128)(2,1)S(1)} %fusion.4), channel_id=1, source_target_pairs={{0,8},{8,0},{16,24},{24,16},{1,9},{9,1},{17,25},{25,17},{2,10},{10... | collective-permute-start | bytes 3145736 | tf_op jit(solution)/shard_map/ppermute | solution.py:192
  705.6 23.7 %collective-permute-start.81 = (bf16[512,1024]{1,0:T(8,128)(2,1)S(1)}, bf16[512,1024]{1,0:T(8,128)(2,1)S(1)}, u32[]{:S(2)}, u32[]{:S(2)}) collective-permute-start(bf16[512,1024]{1,0:T(8,128)(2,1)S(1)} %reduce-precision_convert_fusion.18), channel_id=1, source_target_pairs={{8,16},{16,8},{9,17},{17,9},{10,18},{18,10},{11,19},{19,11},{12,20... | collective-permute-start | bytes 3145736 | tf_op jit(solution)/shard_map/ppermute | solution.py:203
  709.1 44.5 %collective-permute-start.83 = (bf16[256,2816]{1,0:T(8,128)(2,1)}, bf16[256,2816]{1,0:T(8,128)(2,1)}, u32[]{:S(2)}, u32[]{:S(2)}) collective-permute-start(bf16[256,2816]{1,0:T(8,128)(2,1)} %broadcast_select_fusion), channel_id=1, source_target_pairs={{0,2},{2,0},{4,6},{6,4},{1,3},{3,1},{5,7},{7,5},{8,10},{10,8},{12,... | collective-permute-start | bytes 4325384 | tf_op jit(solution)/shard_map/ppermute | solution.py:57
  732.7 38.6 %collective-permute-start.84 = (bf16[512,1024]{1,0:T(8,128)(2,1)}, bf16[512,1024]{1,0:T(8,128)(2,1)}, u32[]{:S(2)}, u32[]{:S(2)}) collective-permute-start(bf16[512,1024]{1,0:T(8,128)(2,1)} %fusion.5), channel_id=1, source_target_pairs={{0,8},{8,0},{16,24},{24,16},{1,9},{9,1},{17,25},{25,17},{2,10},{10... | collective-permute-start | bytes 3145736 | tf_op jit(solution)/shard_map/ppermute | solution.py:192
  736.2 35.2 %collective-permute-start.85 = (bf16[512,1024]{1,0:T(8,128)(2,1)}, bf16[512,1024]{1,0:T(8,128)(2,1)}, u32[]{:S(2)}, u32[]{:S(2)}) collective-permute-start(bf16[512,1024]{1,0:T(8,128)(2,1)} %reduce-precision_convert_fusion.16), channel_id=1, source_target_pairs={{8,16},{16,8},{9,17},{17,9},{10,18},{18,10},{11,19},{19,11},{12,20... | collective-permute-start | bytes 3145736 | tf_op jit(solution)/shard_map/ppermute | solution.py:203
  739.3 43.0 %collective-permute-start.79 = (bf16[256,1024]{1,0:T(8,128)(2,1)}, bf16[256,1024]{1,0:T(8,128)(2,1)}, u32[]{:S(2)}, u32[]{:S(2)}) collective-permute-start(bf16[256,1024]{1,0:T(8,128)(2,1)} %get-tuple-element.1641), channel_id=1, source_target_pairs={{0,1},{1,0},{2,3},{3,2},{4,5},{5,4},{6,7},{7,6},{8,9},{9,8},{10,11... | collective-permute-start | bytes 1572872 | tf_op jit(solution)/shard_map/ppermute | solution.py:62
  775.9 27.4 %collective-permute-start.86 = (bf16[512,1024]{1,0:T(8,128)(2,1)}, bf16[512,1024]{1,0:T(8,128)(2,1)}, u32[]{:S(2)}, u32[]{:S(2)}) collective-permute-start(bf16[512,1024]{1,0:T(8,128)(2,1)} %reduce-precision_convert_fusion.13), channel_id=1, source_target_pairs={{8,0},{16,24},{9,1},{17,25},{10,2},{18,26},{11,3},{19,27},{12,4},{... | collective-permute-start | bytes 3145736 | tf_op jit(solution)/shard_map/ppermute | solution.py:200
  777.2 26.1 %collective-permute-start.87 = (bf16[512,1024]{1,0:T(8,128)(2,1)S(1)}, bf16[512,1024]{1,0:T(8,128)(2,1)}, u32[]{:S(2)}, u32[]{:S(2)}) collective-permute-start(bf16[512,1024]{1,0:T(8,128)(2,1)S(1)} %reduce-precision_convert_fusion.14), channel_id=1, source_target_pairs={{8,16},{16,8},{9,17},{17,9},{10,18},{18,10},{11,19},{19,11},{12,20... | collective-permute-start | bytes 3145736 | tf_op jit(solution)/shard_map/ppermute | solution.py:203
  804.9 28.2 %collective-permute-start.88 = (bf16[512,1024]{1,0:T(8,128)(2,1)S(1)}, bf16[512,1024]{1,0:T(8,128)(2,1)S(1)}, u32[]{:S(2)}, u32[]{:S(2)}) collective-permute-start(bf16[512,1024]{1,0:T(8,128)(2,1)S(1)} %reduce-precision_convert_fusion.12), channel_id=1, source_target_pairs={{8,0},{16,24},{9,1},{17,25},{10,2},{18,26},{11,3},{19,27},{12,4},{... | collective-permute-start | bytes 3145736 | tf_op jit(solution)/shard_map/ppermute | solution.py:200
  (188 other events, 1147.7 us)

commit v2 on v1

--- a/solution.py
+++ b/solution.py
@@ -1078,6 +1078,7 @@
         reps.push(third, g)
     part = do(lambda w, g: mm(w, g, PLAIN, f32, tn=256), wq, gqkv.reshape(3 * Y * S * blk, T))
     part_theirs = at.core(part[blk:])
+    ticks(1)
 
     def first_back(a, b, x, mean, inv, gain, gxn2, z2, gqkv0, gqkv1):
         gxn1 = a + b
@@ -1101,7 +1102,6 @@
     )
     for axis, step in steps2:
         sums = sum_step(sums, axis, step)
-    ticks(1)
     input_grad = do(
         lambda h, grad, z, scale, gain, sums: (
             h + scale * (grad * gain - sums[0:1] / width - z * (sums[1:2] / width))
@@ -1134,8 +1134,8 @@
         small = do(lambda a, b: a + b, small, other)
         return small
 
+    reps.tick(small_step)
     out_kept, out_got = out_step(*out_steps[0])
-    reps.tick(small_step)
     update(1)
     for axis, step in out_steps[1:]:
         out_kept, out_got = out_step(axis, step)
@@ -1147,13 +1147,14 @@
         return adam_update(*a, every.transpose(1, 0, 2).reshape(7, width), 0.3, 0.0)
 
     mn, vn, wn = do(norm_update, small_all, norm_params, m_norm, v_norm)
+    update(1)
+    ticks(1)
     update(2)
-    ticks(1)
-    update(1)
     out_cols = do(
         lambda h, a, b: (h + (a.astype(f32) + b.astype(f32))).astype(bf16), hidden, out_kept, out_got
     )
     block_output = to_rows(out_cols)
+    update(2)
     while reps.busy():
         reps.tick()
         update(2)

time: 855 us -> 854 us (level)
  waiting for transfers between devices: 264 us -> 250 us
  blocking collectives: 0 us -> 11.9 us
    all_to_all x0 -> x1, blocking collectives: none -> 11.9 us  [to_rows(): got = lax.all_to_all(split, plane, split_axis=0, concat_axis=0, tiled=True)]
  transfers between devices with their start and end apart: 96 -> 95, of which waited for: 49 -> 47; matrix products, arithmetic and copies ran while one was open for 16% -> 17% of each run, Pallas kernels for 21% -> 22%
where the time goes in v2:
time: 854 us; the launch traced here: 840 us
  waiting for transfers between devices  250 us (29%)
  Pallas kernels  213 us (25%)
  starting transfers between devices  140 us (16%)
  local copies, waits for them, and re-layouts  94.2 us (11%)
  other arithmetic  88.8 us (10%)
  matrix products  38 us (4%)
  blocking collectives  11.9 us (1%)
    ppermute x21, waiting for transfers between devices, along(): return lax.ppermute(x, 'shard', [(i, i ^ step) for i in range(self.s_size)])  112 us
    pallas_call x9, Pallas kernels, adam_part(): pl.pallas_call(functools.partial(adam_kernel, rate, two), grid_spec=pltpu...  68.7 us
    unnamed x280, local copies, waits for them, and re-layouts  53.5 us
    ppermute x6, waiting for transfers between devices, tick(): slot['in_got'] = lax.ppermute(out['new'], 'rep', [(0, 1), (3, 2)])  49.7 us
    pallas_call x12, Pallas kernels, mm(): pl.pallas_call(functools.partial(product_kernel, dims), grid=(m // tm, n...  47 us
    dot_general x18, matrix products, dot(): return lax.dot_general(a, b, dims, preferred_element_type=f32)  38 us
    convert_element_type x16, other arithmetic, add(): lax.reduce_precision(a.astype(f32) + b.astype(f32), 8, 7).astype(bf16)  33.5 us
    ppermute x21, waiting for transfers between devices, along(): lax.ppermute(x, 'ctx', [(i, i ^ 2 * step) for i in range(self.ctx_size)])  33.5 us
  transfers between devices with their start and end apart: 95, of which 47 were waited for; matrix products, arithmetic and copies ran while one was open for 17% of the time, Pallas kernels for 22%

profile of v2, /device:TPU:0, one launch (start us, length us, event | category | flops | bytes accessed | tf_op | source)
XLA Modules:
  0.0 839.9 jit_solution(6128142822345135897)
XLA Ops:
  12.9 4.8 all-to-all-start
  72.8 11.1 %collective-permute-done.5.b_ref.d_ref = bf16[1536,512]{1,0:T(8,128)(2,1)} collective-permute-done((bf16[1536,512]{1,0:T(8,128)(2,1)}, bf16[1536,512]{1,0:T(8,128)(2,1)}, u32[]{:S(2)}, u32[]{:S(2)}) %collective-permute-start.5) | collective-permute-done | bytes 1572896 | tf_op jit(solution)/shard_map/ppermute | solution.py:62
  102.0 10.7 %collective-permute-done.6 = bf16[768,512]{1,0:T(8,128)(2,1)S(1)} collective-permute-done((bf16[768,512]{1,0:T(8,128)(2,1)S(1)}, bf16[768,512]{1,0:T(8,128)(2,1)S(1)}, u32[]{:S(2)}, u32[]{:S(2)}) %collective-permute-start.6) | collective-permute-done | bytes 786464 | tf_op jit(solution)/shard_map/ppermute | solution.py:61
  126.1 4.6 shard_map.316
  151.0 8.7 %collective-permute-done.13.b_ref.d_ref = bf16[512,512]{1,0:T(8,128)(2,1)} collective-permute-done((bf16[512,512]{1,0:T(8,128)(2,1)}, bf16[512,512]{1,0:T(8,128)(2,1)}, u32[]{:S(2)}, u32[]{:S(2)}) %collective-permute-start.13) | collective-permute-done | bytes 524320 | tf_op jit(solution)/shard_map/ppermute | solution.py:62
  167.4 4.9 collective-permute-done.18
  199.8 5.1 convolution_convert_fusion.1.a_ref.c_ref
  218.3 5.1 shard_map.324.b_ref.x_ref
  225.5 5.5 shard_map.325.grad_ref
  240.5 13.7 %collective-permute-done.24 = f32[4,2,1,704]{3,0,2,1:T(4,128)S(1)} collective-permute-done((f32[4,2,1,704]{3,0,2,1:T(4,128)S(1)}, f32[4,2,1,704]{3,0,2,1:T(4,128)S(1)}, u32[]{:S(2)}, u32[]{:S(2)}) %collective-permute-start.24) | collective-permute-done | bytes 22560 | tf_op jit(solution)/shard_map/ppermute | solution.py:62
  257.5 8.2 collective-permute-done.27
  276.8 29.4 %collective-permute-done.30.ub_ref = bf16[704,1024]{1,0:T(8,128)(2,1)S(1)} collective-permute-done((bf16[704,1024]{1,0:T(8,128)(2,1)S(1)}, bf16[704,1024]{1,0:T(8,128)(2,1)S(1)}, u32[]{:S(2)}, u32[]{:S(2)}) %collective-permute-start.30) | collective-permute-done | bytes 1441824 | tf_op jit(solution)/shard_map/ppermute | solution.py:62
  308.4 7.5 shard_map.331
  319.9 5.4 shard_map.332
  337.9 21.2 %collective-permute-done.36 = bf16[352,2048]{1,0:T(8,128)(2,1)S(1)} collective-permute-done((bf16[352,2048]{1,0:T(8,128)(2,1)S(1)}, bf16[352,2048]{1,0:T(8,128)(2,1)S(1)}, u32[]{:S(2)}, u32[]{:S(2)}) %collective-permute-start.36) | collective-permute-done | bytes 1441824 | tf_op jit(solution)/shard_map/ppermute | solution.py:197
  370.6 4.8 collective-permute-start.44
  377.2 5.7 shard_map.334
  387.7 5.8 shard_map.335
  393.5 5.3 shard_map.336
  398.8 7.2 collective-permute-done.44
  411.3 5.9 collective-permute-done.42.got0_ref
  421.4 5.2 convolution_add_fusion.2
  436.3 5.9 shard_map.338
  442.5 17.7 %collective-permute-done.51 = bf16[256,2816]{1,0:T(8,128)(2,1)S(1)} collective-permute-done((bf16[256,2816]{1,0:T(8,128)(2,1)S(1)}, bf16[256,2816]{1,0:T(8,128)(2,1)S(1)}, u32[]{:S(2)}, u32[]{:S(2)}) %collective-permute-start.51) | collective-permute-done | bytes 1441824 | tf_op jit(solution)/shard_map/ppermute | solution.py:197
  471.2 6.4 collective-permute-done.49.got0_ref
  483.6 4.5 collective-permute-start.57
  496.9 5.5 shard_map.340
  502.4 5.5 shard_map.341
  511.4 7.8 shard_map.344
  537.6 5.2 collective-permute-done.56
  544.1 8.2 shard_map.345
  554.8 10.8 %collective-permute-done.62 = bf16[256,2816]{1,0:T(8,128)(2,1)S(1)} collective-permute-done((bf16[256,2816]{1,0:T(8,128)(2,1)S(1)}, bf16[256,2816]{1,0:T(8,128)(2,1)S(1)}, u32[]{:S(2)}, u32[]{:S(2)}) %collective-permute-start.62) | collective-permute-done | bytes 1441824 | tf_op jit(solution)/shard_map/ppermute | solution.py:192
  573.1 13.7 %collective-permute-done.60.got0_ref = bf16[2,1,768,512]{3,2,1,0:T(8,128)(2,1)S(1)} collective-permute-done((bf16[2,1,768,512]{3,2,1,0:T(8,128)(2,1)S(1)}, bf16[2,1,768,512]{3,2,1,0:T(8,128)(2,1)S(1)}, u32[]{:S(2)}, u32[]{:S(2)}) %collective-permute-start.60) | collective-permute-done | bytes 1572896 | tf_op jit(solution)/shard_map/ppermute | solution.py:62
  587.6 9.1 %shard_map.346 = bf16[3,2,2,256,1024]{4,3,2,1,0:T(8,128)(2,1)} custom-call(s32[4]{0:T(128)S(1)} %pad_add_fusion.1.bits_ref, bf16[2,1,768,512]{3,2,1,0:T(8,128)(2,1)S(1)} %pad_maximum_fusion.1.own0_ref, bf16[2,1,768,512]{3,2,1,0:T(8,128)(2,1)S(1)} %collective-permute-done.60.got0_ref, bf16[1,2,768,512]{3,2,1,0:T(8,128)(2,1)S(1)} %pad_maximum_fusion.2.own1_ref, ...), custom_call_target="tpu_custom_call" | custom-call | flops 1024 | bytes 1024 | tf_op jit(solution)/shard_map/pallas_call | solution.py:409
  596.8 5.7 fusion.31
  610.8 9.2 %collective-permute-start.67 = (bf16[512,1024]{1,0:T(8,128)(2,1)}, bf16[512,1024]{1,0:T(8,128)(2,1)}, u32[]{:S(2)}, u32[]{:S(2)}) collective-permute-start(bf16[512,1024]{1,0:T(8,128)(2,1)} %pad_maximum_fusion.10), channel_id=1, source_target_pairs={{0,8},{24,16},{1,9},{25,17},{2,10},{26,18},{3,11},{27,19},{4,12},{... | collective-permute-start | bytes 3145736 | tf_op jit(solution)/shard_map/ppermute | solution.py:197
  620.0 4.3 constant_dynamic-slice_fusion
  628.8 6.0 shard_map.350
  658.2 8.8 %collective-permute-start.71 = (bf16[512,1024]{1,0:T(8,128)(2,1)}, bf16[512,1024]{1,0:T(8,128)(2,1)}, u32[]{:S(2)}, u32[]{:S(2)}) collective-permute-start(bf16[512,1024]{1,0:T(8,128)(2,1)} %shard_map.347), channel_id=1, source_target_pairs={{0,8},{24,16},{1,9},{25,17},{2,10},{26,18},{3,11},{27,19},{4,12},{... | collective-permute-start | bytes 3145736 | tf_op jit(solution)/shard_map/ppermute | solution.py:197
  673.6 4.3 all-to-all-start.1
  681.1 6.1 all-to-all-done.1
  705.6 13.2 %shard_map.352 = (f32[256,11264]{1,0:T(8,128)}, f32[256,11264]{1,0:T(8,128)}, f32[256,11264]{1,0:T(8,128)}) custom-call(s32[1]{0:T(128)} %bitcast.8.core_ref, f32[256,11264]{1,0:T(8,128)} %w_ref.9, f32[256,11264]{1,0:T(8,128)} %m_ref.3, f32[256,11264]{1,0:T(8,128)} %v_ref.3, bf16[256,2816]{1,0:T(8,128)(2,1)S(1)} %broadcast_select_fusion.3.refs_0_, ...), custom_call_target="tpu_custom_call" | custom-call | flops 1024 | bytes 1024 | tf_op jit(solution)/shard_map/pallas_call | solution.py:520
  747.5 14.1 %shard_map.354 = (f32[256,11264]{1,0:T(8,128)}, f32[256,11264]{1,0:T(8,128)}, f32[256,11264]{1,0:T(8,128)}) custom-call(s32[1]{0:T(128)} %bitcast.8.core_ref, f32[256,11264]{1,0:T(8,128)} %w_ref.9, f32[256,11264]{1,0:T(8,128)} %m_ref.3, f32[256,11264]{1,0:T(8,128)} %v_ref.3, ...), custom_call_target="tpu_custom_call", output_to_operand_aliasing={{0}: (6, {}), {1}: (7, {}), {2}: (8, {})} | custom-call | flops 1024 | bytes 1024 | tf_op jit(solution)/shard_map/pallas_call | solution.py:520
  781.3 11.9 %all_to_all.20 = bf16[8,256,128]{2,1,0:T(8,128)(2,1)S(1)} all-to-all(bf16[8,256,128]{2,1,0:T(8,128)(2,1)S(1)} %bitcast.200), channel_id=1, replica_groups=mesh['rep'=4,'ctx'=4,'shard'=2] {'ctx','shard'}, dimensions={0} | all-to-all | bytes 1048576 | tf_op jit(solution)/shard_map/all_to_all | solution.py:1119
  794.2 6.2 shard_map.357
  807.1 6.2 shard_map.358
  813.3 18.0 %collective-permute-done.89 = bf16[512,1024]{1,0:T(8,128)(2,1)S(1)} collective-permute-done((bf16[512,1024]{1,0:T(8,128)(2,1)S(1)}, bf16[512,1024]{1,0:T(8,128)(2,1)S(1)}, u32[]{:S(2)}, u32[]{:S(2)}) %collective-permute-start.89) | collective-permute-done | bytes 1048608 | tf_op jit(solution)/shard_map/ppermute | solution.py:200
  833.4 6.2 shard_map.359
  (674 shorter events, 430.9 us)
Async XLA Ops:
  46.2 37.7 %collective-permute-start.5 = (bf16[1536,512]{1,0:T(8,128)(2,1)}, bf16[1536,512]{1,0:T(8,128)(2,1)}, u32[]{:S(2)}, u32[]{:S(2)}) collective-permute-start(bf16[1536,512]{1,0:T(8,128)(2,1)} %convolution_convert_fusion.7), channel_id=1, source_target_pairs={{0,1},{1,0},{2,3},{3,2},{4,5},{5,4},{6,7},{7,6},{8,9},{9,8},{10,11... | collective-permute-start | bytes 4718600 | tf_op jit(solution)/shard_map/ppermute | solution.py:62
  47.5 40.4 %collective-permute-start.9 = (bf16[1536,512]{1,0:T(8,128)(2,1)}, bf16[1536,512]{1,0:T(8,128)(2,1)}, u32[]{:S(2)}, u32[]{:S(2)}) collective-permute-start(bf16[1536,512]{1,0:T(8,128)(2,1)} %convolution_convert_fusion.6), channel_id=1, source_target_pairs={{0,4},{2,6},{4,0},{6,2},{1,5},{3,7},{5,1},{7,3},{8,12},{10,14},{12... | collective-permute-start | bytes 4718600 | tf_op jit(solution)/shard_map/ppermute | solution.py:61
  63.7 30.3 %collective-permute-start.7 = (bf16[2,1,64,2048]{3,2,1,0:T(8,128)(2,1)}, bf16[2,1,64,2048]{3,2,1,0:T(8,128)(2,1)}, u32[]{:S(2)}, u32[]{:S(2)}) collective-permute-start(bf16[2,1,64,2048]{3,2,1,0:T(8,128)(2,1)} %pad_maximum_fusion.12), channel_id=1, source_target_pairs={{0,1},{1,0},{2,3},{3,2},{4,5},{5,4},{6,7},{7,6},{8,9},{9,8},{10,11... | collective-permute-start | bytes 1572872 | tf_op jit(solution)/shard_map/ppermute | solution.py:62
  64.6 30.1 %collective-permute-start.8 = (bf16[1,2,64,2048]{3,2,1,0:T(8,128)(2,1)}, bf16[1,2,64,2048]{3,2,1,0:T(8,128)(2,1)}, u32[]{:S(2)}, u32[]{:S(2)}) collective-permute-start(bf16[1,2,64,2048]{3,2,1,0:T(8,128)(2,1)} %pad_maximum_fusion.13), channel_id=1, source_target_pairs={{0,4},{2,6},{4,0},{6,2},{1,5},{3,7},{5,1},{7,3},{8,12},{10,14},{12... | collective-permute-start | bytes 1572872 | tf_op jit(solution)/shard_map/ppermute | solution.py:61
  96.3 27.0 %collective-permute-start.11 = (bf16[768,512]{1,0:T(8,128)(2,1)}, bf16[768,512]{1,0:T(8,128)(2,1)}, u32[]{:S(2)}, u32[]{:S(2)}) collective-permute-start(bf16[768,512]{1,0:T(8,128)(2,1)} %get-tuple-element.1051), channel_id=1, source_target_pairs={{0,1},{1,0},{2,3},{3,2},{4,5},{5,4},{6,7},{7,6},{8,9},{9,8},{10,11... | collective-permute-start | bytes 2359304 | tf_op jit(solution)/shard_map/ppermute | solution.py:62
  188.9 77.6 %collective-permute-start.23 = (bf16[1408,1024]{1,0:T(8,128)(2,1)}, bf16[1408,1024]{1,0:T(8,128)(2,1)}, u32[]{:S(2)}, u32[]{:S(2)}) collective-permute-start(bf16[1408,1024]{1,0:T(8,128)(2,1)} %convolution_convert_fusion.3), channel_id=1, source_target_pairs={{0,1},{1,0},{2,3},{3,2},{4,5},{5,4},{6,7},{7,6},{8,9},{9,8},{10,11... | collective-permute-start | bytes 8650760 | tf_op jit(solution)/shard_map/ppermute | solution.py:62
  193.0 76.5 %collective-permute-start.29 = (bf16[1408,1024]{1,0:T(8,128)(2,1)}, bf16[1408,1024]{1,0:T(8,128)(2,1)}, u32[]{:S(2)}, u32[]{:S(2)}) collective-permute-start(bf16[1408,1024]{1,0:T(8,128)(2,1)} %convolution_convert_fusion.2), channel_id=1, source_target_pairs={{0,4},{2,6},{4,0},{6,2},{1,5},{3,7},{5,1},{7,3},{8,12},{10,14},{12... | collective-permute-start | bytes 8650760 | tf_op jit(solution)/shard_map/ppermute | solution.py:61
  196.8 57.4 %collective-permute-start.24 = (f32[4,2,1,704]{3,0,2,1:T(4,128)S(1)}, f32[4,2,1,704]{3,0,2,1:T(4,128)S(1)}, u32[]{:S(2)}, u32[]{:S(2)}) collective-permute-start(f32[4,2,1,704]{3,0,2,1:T(4,128)S(1)} %constant_dynamic-slice_fusion.4), channel_id=1, source_target_pairs={{0,1},{1,0},{2,3},{3,2},{4,5},{5,4},{6,7},{7,6},{8,9},{9,8},{10,11... | collective-permute-start | bytes 67592 | tf_op jit(solution)/shard_map/ppermute | solution.py:62
  274.2 32.0 %collective-permute-start.30 = (bf16[704,1024]{1,0:T(8,128)(2,1)S(1)}, bf16[704,1024]{1,0:T(8,128)(2,1)S(1)}, u32[]{:S(2)}, u32[]{:S(2)}) collective-permute-start(bf16[704,1024]{1,0:T(8,128)(2,1)S(1)} %get-tuple-element.1255), channel_id=1, source_target_pairs={{0,1},{1,0},{2,3},{3,2},{4,5},{5,4},{6,7},{7,6},{8,9},{9,8},{10,11... | collective-permute-start | bytes 4325384 | tf_op jit(solution)/shard_map/ppermute | solution.py:62
  275.1 31.7 %collective-permute-start.28 = (bf16[704,1024]{1,0:T(8,128)(2,1)S(1)}, bf16[704,1024]{1,0:T(8,128)(2,1)S(1)}, u32[]{:S(2)}, u32[]{:S(2)}) collective-permute-start(bf16[704,1024]{1,0:T(8,128)(2,1)S(1)} %get-tuple-element.1245), channel_id=1, source_target_pairs={{0,4},{2,6},{4,0},{6,2},{1,5},{3,7},{5,1},{7,3},{8,12},{10,14},{12... | collective-permute-start | bytes 4325384 | tf_op jit(solution)/shard_map/ppermute | solution.py:61
  327.8 31.3 %collective-permute-start.36 = (bf16[352,2048]{1,0:T(8,128)(2,1)S(1)}, bf16[352,2048]{1,0:T(8,128)(2,1)S(1)}, u32[]{:S(2)}, u32[]{:S(2)}) collective-permute-start(bf16[352,2048]{1,0:T(8,128)(2,1)S(1)} %get-tuple-element.1300), channel_id=1, source_target_pairs={{0,8},{24,16},{1,9},{25,17},{2,10},{26,18},{3,11},{27,19},{4,12},{... | collective-permute-start | bytes 4325384 | tf_op jit(solution)/shard_map/ppermute | solution.py:197
  334.6 29.9 %collective-permute-start.34 = (bf16[2,1,704,512]{3,2,1,0:T(8,128)(2,1)S(1)}, bf16[2,1,704,512]{3,2,1,0:T(8,128)(2,1)S(1)}, u32[]{:S(2)}, u32[]{:S(2)}) collective-permute-start(bf16[2,1,704,512]{3,2,1,0:T(8,128)(2,1)S(1)} %pad_maximum_fusion.3.own0_ref), channel_id=1, source_target_pairs={{0,1},{1,0},{2,3},{3,2},{4,5},{5,4},{6,7},{7,6},{8,9},{9,8},{10,11... | collective-permute-start | bytes 4325384 | tf_op jit(solution)/shard_map/ppermute | solution.py:62
  335.8 29.6 %collective-permute-start.35 = (bf16[1,2,704,512]{3,2,1,0:T(8,128)(2,1)S(1)}, bf16[1,2,704,512]{3,2,1,0:T(8,128)(2,1)S(1)}, u32[]{:S(2)}, u32[]{:S(2)}) collective-permute-start(bf16[1,2,704,512]{3,2,1,0:T(8,128)(2,1)S(1)} %pad_maximum_fusion.4.own1_ref), channel_id=1, source_target_pairs={{0,4},{2,6},{4,0},{6,2},{1,5},{3,7},{5,1},{7,3},{8,12},{10,14},{12... | collective-permute-start | bytes 4325384 | tf_op jit(solution)/shard_map/ppermute | solution.py:61
  336.2 32.8 %collective-permute-start.37 = (f32[2,1024]{1,0:T(2,128)S(1)}, f32[2,1024]{1,0:T(2,128)S(1)}, u32[]{:S(2)}, u32[]{:S(2)}) collective-permute-start(f32[2,1024]{1,0:T(2,128)S(1)} %add.401), channel_id=1, source_target_pairs={{0,4},{2,6},{4,0},{6,2},{1,5},{3,7},{5,1},{7,3},{8,12},{10,14},{12... | collective-permute-start | bytes 24584 | tf_op jit(solution)/shard_map/ppermute | solution.py:61
  370.6 35.4 %collective-permute-start.44 = (bf16[352,2048]{1,0:T(8,128)(2,1)}, bf16[352,2048]{1,0:T(8,128)(2,1)}, u32[]{:S(2)}, u32[]{:S(2)}) collective-permute-start(bf16[352,2048]{1,0:T(8,128)(2,1)} %get-tuple-element.1353), channel_id=1, source_target_pairs={{0,8},{24,16},{1,9},{25,17},{2,10},{26,18},{3,11},{27,19},{4,12},{... | collective-permute-start | bytes 4325384 | tf_op jit(solution)/shard_map/ppermute | solution.py:197
  375.3 30.6 %collective-permute-start.45 = (bf16[352,2048]{1,0:T(8,128)(2,1)}, bf16[352,2048]{1,0:T(8,128)(2,1)}, u32[]{:S(2)}, u32[]{:S(2)}) collective-permute-start(bf16[352,2048]{1,0:T(8,128)(2,1)} %reduce-precision_convert_fusion.11), channel_id=1, source_target_pairs={{8,16},{16,8},{9,17},{17,9},{10,18},{18,10},{11,19},{19,11},{12,20... | collective-permute-start | bytes 4325384 | tf_op jit(solution)/shard_map/ppermute | solution.py:203
  383.4 33.8 %collective-permute-start.42 = (bf16[2,1,704,512]{3,2,1,0:T(8,128)(2,1)S(1)}, bf16[2,1,704,512]{3,2,1,0:T(8,128)(2,1)S(1)}, u32[]{:S(2)}, u32[]{:S(2)}) collective-permute-start(bf16[2,1,704,512]{3,2,1,0:T(8,128)(2,1)S(1)} %pad_maximum_fusion.5.own0_ref), channel_id=1, source_target_pairs={{0,1},{1,0},{2,3},{3,2},{4,5},{5,4},{6,7},{7,6},{8,9},{9,8},{10,11... | collective-permute-start | bytes 4325384 | tf_op jit(solution)/shard_map/ppermute | solution.py:62
  384.4 33.4 %collective-permute-start.43 = (bf16[1,2,704,512]{3,2,1,0:T(8,128)(2,1)S(1)}, bf16[1,2,704,512]{3,2,1,0:T(8,128)(2,1)S(1)}, u32[]{:S(2)}, u32[]{:S(2)}) collective-permute-start(bf16[1,2,704,512]{3,2,1,0:T(8,128)(2,1)S(1)} %pad_maximum_fusion.6.own1_ref), channel_id=1, source_target_pairs={{0,4},{2,6},{4,0},{6,2},{1,5},{3,7},{5,1},{7,3},{8,12},{10,14},{12... | collective-permute-start | bytes 4325384 | tf_op jit(solution)/shard_map/ppermute | solution.py:61
  428.0 32.2 %collective-permute-start.51 = (bf16[256,2816]{1,0:T(8,128)(2,1)S(1)}, bf16[256,2816]{1,0:T(8,128)(2,1)S(1)}, u32[]{:S(2)}, u32[]{:S(2)}) collective-permute-start(bf16[256,2816]{1,0:T(8,128)(2,1)S(1)} %copy-done.120), channel_id=1, source_target_pairs={{0,8},{24,16},{1,9},{25,17},{2,10},{26,18},{3,11},{27,19},{4,12},{... | collective-permute-start | bytes 4325384 | tf_op jit(solution)/shard_map/ppermute | solution.py:197
  429.9 34.5 %collective-permute-start.52 = (bf16[352,2048]{1,0:T(8,128)(2,1)S(1)}, bf16[352,2048]{1,0:T(8,128)(2,1)S(1)}, u32[]{:S(2)}, u32[]{:S(2)}) collective-permute-start(bf16[352,2048]{1,0:T(8,128)(2,1)S(1)} %reduce-precision_convert_fusion.9), channel_id=1, source_target_pairs={{8,0},{16,24},{9,1},{17,25},{10,2},{18,26},{11,3},{19,27},{12,4},{... | collective-permute-start | bytes 4325384 | tf_op jit(solution)/shard_map/ppermute | solution.py:200
  431.2 33.3 %collective-permute-start.53 = (bf16[352,2048]{1,0:T(8,128)(2,1)S(1)}, bf16[352,2048]{1,0:T(8,128)(2,1)S(1)}, u32[]{:S(2)}, u32[]{:S(2)}) collective-permute-start(bf16[352,2048]{1,0:T(8,128)(2,1)S(1)} %reduce-precision_convert_fusion.10), channel_id=1, source_target_pairs={{8,16},{16,8},{9,17},{17,9},{10,18},{18,10},{11,19},{19,11},{12,20... | collective-permute-start | bytes 4325384 | tf_op jit(solution)/shard_map/ppermute | solution.py:203
  483.6 36.2 %collective-permute-start.57 = (bf16[256,2816]{1,0:T(8,128)(2,1)}, bf16[256,2816]{1,0:T(8,128)(2,1)S(1)}, u32[]{:S(2)}, u32[]{:S(2)}) collective-permute-start(bf16[256,2816]{1,0:T(8,128)(2,1)} %get-tuple-element.1463), channel_id=1, source_target_pairs={{0,8},{24,16},{1,9},{25,17},{2,10},{26,18},{3,11},{27,19},{4,12},{... | collective-permute-start | bytes 4325384 | tf_op jit(solution)/shard_map/ppermute | solution.py:197
  488.1 35.8 %collective-permute-start.58 = (bf16[352,2048]{1,0:T(8,128)(2,1)}, bf16[352,2048]{1,0:T(8,128)(2,1)S(1)}, u32[]{:S(2)}, u32[]{:S(2)}) collective-permute-start(bf16[352,2048]{1,0:T(8,128)(2,1)} %reduce-precision_convert_fusion.7), channel_id=1, source_target_pairs={{8,0},{16,24},{9,1},{17,25},{10,2},{18,26},{11,3},{19,27},{12,4},{... | collective-permute-start | bytes 4325384 | tf_op jit(solution)/shard_map/ppermute | solution.py:200
  489.4 34.5 %collective-permute-start.59 = (bf16[256,2816]{1,0:T(8,128)(2,1)}, bf16[256,2816]{1,0:T(8,128)(2,1)}, u32[]{:S(2)}, u32[]{:S(2)}) collective-permute-start(bf16[256,2816]{1,0:T(8,128)(2,1)} %reduce-precision_convert_fusion.8), channel_id=1, source_target_pairs={{8,16},{16,8},{9,17},{17,9},{10,18},{18,10},{11,19},{19,11},{12,20... | collective-permute-start | bytes 4325384 | tf_op jit(solution)/shard_map/ppermute | solution.py:203
  531.4 34.2 %collective-permute-start.62 = (bf16[256,2816]{1,0:T(8,128)(2,1)S(1)}, bf16[256,2816]{1,0:T(8,128)(2,1)S(1)}, u32[]{:S(2)}, u32[]{:S(2)}) collective-permute-start(bf16[256,2816]{1,0:T(8,128)(2,1)S(1)} %fusion), channel_id=1, source_target_pairs={{0,8},{8,0},{16,24},{24,16},{1,9},{9,1},{17,25},{25,17},{2,10},{10... | collective-permute-start | bytes 4325384 | tf_op jit(solution)/shard_map/ppermute | solution.py:192
  535.3 30.3 %collective-permute-start.63 = (bf16[256,2816]{1,0:T(8,128)(2,1)S(1)}, bf16[256,2816]{1,0:T(8,128)(2,1)}, u32[]{:S(2)}, u32[]{:S(2)}) collective-permute-start(bf16[256,2816]{1,0:T(8,128)(2,1)S(1)} %reduce-precision_convert_fusion.6), channel_id=1, source_target_pairs={{8,16},{16,8},{9,17},{17,9},{10,18},{18,10},{11,19},{19,11},{12,20... | collective-permute-start | bytes 4325384 | tf_op jit(solution)/shard_map/ppermute | solution.py:203
  552.3 34.5 %collective-permute-start.60 = (bf16[2,1,768,512]{3,2,1,0:T(8,128)(2,1)S(1)}, bf16[2,1,768,512]{3,2,1,0:T(8,128)(2,1)S(1)}, u32[]{:S(2)}, u32[]{:S(2)}) collective-permute-start(bf16[2,1,768,512]{3,2,1,0:T(8,128)(2,1)S(1)} %pad_maximum_fusion.1.own0_ref), channel_id=1, source_target_pairs={{0,1},{1,0},{2,3},{3,2},{4,5},{5,4},{6,7},{7,6},{8,9},{9,8},{10,11... | collective-permute-start | bytes 4718600 | tf_op jit(solution)/shard_map/ppermute | solution.py:62
  553.3 34.3 %collective-permute-start.61 = (bf16[1,2,768,512]{3,2,1,0:T(8,128)(2,1)S(1)}, bf16[1,2,768,512]{3,2,1,0:T(8,128)(2,1)}, u32[]{:S(2)}, u32[]{:S(2)}) collective-permute-start(bf16[1,2,768,512]{3,2,1,0:T(8,128)(2,1)S(1)} %pad_maximum_fusion.2.own1_ref), channel_id=1, source_target_pairs={{0,4},{2,6},{4,0},{6,2},{1,5},{3,7},{5,1},{7,3},{8,12},{10,14},{12... | collective-permute-start | bytes 4718600 | tf_op jit(solution)/shard_map/ppermute | solution.py:61
  569.1 35.6 %collective-permute-start.64 = (bf16[256,2816]{1,0:T(8,128)(2,1)S(1)}, bf16[256,2816]{1,0:T(8,128)(2,1)S(1)}, u32[]{:S(2)}, u32[]{:S(2)}) collective-permute-start(bf16[256,2816]{1,0:T(8,128)(2,1)S(1)} %fusion.1), channel_id=1, source_target_pairs={{0,8},{8,0},{16,24},{24,16},{1,9},{9,1},{17,25},{25,17},{2,10},{10... | collective-permute-start | bytes 4325384 | tf_op jit(solution)/shard_map/ppermute | solution.py:192
  572.3 32.4 %collective-permute-start.65 = (bf16[256,2816]{1,0:T(8,128)(2,1)S(1)}, bf16[256,2816]{1,0:T(8,128)(2,1)S(1)}, u32[]{:S(2)}, u32[]{:S(2)}) collective-permute-start(bf16[256,2816]{1,0:T(8,128)(2,1)S(1)} %reduce-precision_convert_fusion.4), channel_id=1, source_target_pairs={{8,16},{16,8},{9,17},{17,9},{10,18},{18,10},{11,19},{19,11},{12,20... | collective-permute-start | bytes 4325384 | tf_op jit(solution)/shard_map/ppermute | solution.py:203
  607.7 33.4 %collective-permute-start.68 = (bf16[256,2816]{1,0:T(8,128)(2,1)}, bf16[256,2816]{1,0:T(8,128)(2,1)}, u32[]{:S(2)}, u32[]{:S(2)}) collective-permute-start(bf16[256,2816]{1,0:T(8,128)(2,1)} %reduce-precision_convert_fusion.1), channel_id=1, source_target_pairs={{8,0},{16,24},{9,1},{17,25},{10,2},{18,26},{11,3},{19,27},{12,4},{... | collective-permute-start | bytes 4325384 | tf_op jit(solution)/shard_map/ppermute | solution.py:200
  609.0 32.2 %collective-permute-start.69 = (bf16[256,2816]{1,0:T(8,128)(2,1)}, bf16[256,2816]{1,0:T(8,128)(2,1)}, u32[]{:S(2)}, u32[]{:S(2)}) collective-permute-start(bf16[256,2816]{1,0:T(8,128)(2,1)} %reduce-precision_convert_fusion.2), channel_id=1, source_target_pairs={{8,16},{16,8},{9,17},{17,9},{10,18},{18,10},{11,19},{19,11},{12,20... | collective-permute-start | bytes 4325384 | tf_op jit(solution)/shard_map/ppermute | solution.py:203
  610.8 27.6 %collective-permute-start.67 = (bf16[512,1024]{1,0:T(8,128)(2,1)}, bf16[512,1024]{1,0:T(8,128)(2,1)}, u32[]{:S(2)}, u32[]{:S(2)}) collective-permute-start(bf16[512,1024]{1,0:T(8,128)(2,1)} %pad_maximum_fusion.10), channel_id=1, source_target_pairs={{0,8},{24,16},{1,9},{25,17},{2,10},{26,18},{3,11},{27,19},{4,12},{... | collective-permute-start | bytes 3145736 | tf_op jit(solution)/shard_map/ppermute | solution.py:197
  624.3 74.2 %collective-permute-start.41 = (bf16[1024,1024]{1,0:T(8,128)(2,1)}, bf16[1024,1024]{1,0:T(8,128)(2,1)}, u32[]{:S(2)}, u32[]{:S(2)}) collective-permute-start(bf16[1024,1024]{1,0:T(8,128)(2,1)} %bitcast.55), channel_id=1, source_target_pairs={{0,2},{2,0},{4,6},{6,4},{1,3},{3,1},{5,7},{7,5},{8,10},{10,8},{12,... | collective-permute-start | bytes 6291464 | tf_op jit(solution)/shard_map/ppermute | solution.py:57
  647.5 44.4 %collective-permute-start.72 = (bf16[256,2816]{1,0:T(8,128)(2,1)}, bf16[256,2816]{1,0:T(8,128)(2,1)}, u32[]{:S(2)}, u32[]{:S(2)}) collective-permute-start(bf16[256,2816]{1,0:T(8,128)(2,1)} %reduce-precision_convert_fusion), channel_id=1, source_target_pairs={{8,0},{16,24},{9,1},{17,25},{10,2},{18,26},{11,3},{19,27},{12,4},{... | collective-permute-start | bytes 4325384 | tf_op jit(solution)/shard_map/ppermute | solution.py:200
  658.2 31.2 %collective-permute-start.71 = (bf16[512,1024]{1,0:T(8,128)(2,1)}, bf16[512,1024]{1,0:T(8,128)(2,1)}, u32[]{:S(2)}, u32[]{:S(2)}) collective-permute-start(bf16[512,1024]{1,0:T(8,128)(2,1)} %shard_map.347), channel_id=1, source_target_pairs={{0,8},{24,16},{1,9},{25,17},{2,10},{26,18},{3,11},{27,19},{4,12},{... | collective-permute-start | bytes 3145736 | tf_op jit(solution)/shard_map/ppermute | solution.py:197
  667.0 24.9 %collective-permute-start.73 = (bf16[512,1024]{1,0:T(8,128)(2,1)}, bf16[512,1024]{1,0:T(8,128)(2,1)}, u32[]{:S(2)}, u32[]{:S(2)}) collective-permute-start(bf16[512,1024]{1,0:T(8,128)(2,1)} %reduce-precision_convert_fusion.19), channel_id=1, source_target_pairs={{8,16},{16,8},{9,17},{17,9},{10,18},{18,10},{11,19},{19,11},{12,20... | collective-permute-start | bytes 3145736 | tf_op jit(solution)/shard_map/ppermute | solution.py:203
  680.6 25.0 %collective-permute-start.78 = (bf16[256,2816]{1,0:T(8,128)(2,1)}, bf16[256,2816]{1,0:T(8,128)(2,1)}, u32[]{:S(2)}, u32[]{:S(2)}) collective-permute-start(bf16[256,2816]{1,0:T(8,128)(2,1)} %broadcast_select_fusion.2), channel_id=1, source_target_pairs={{0,2},{2,0},{4,6},{6,4},{1,3},{3,1},{5,7},{7,5},{8,10},{10,8},{12,... | collective-permute-start | bytes 4325384 | tf_op jit(solution)/shard_map/ppermute | solution.py:57
  696.4 30.8 %collective-permute-start.80 = (bf16[512,1024]{1,0:T(8,128)(2,1)S(1)}, bf16[512,1024]{1,0:T(8,128)(2,1)S(1)}, u32[]{:S(2)}, u32[]{:S(2)}) collective-permute-start(bf16[512,1024]{1,0:T(8,128)(2,1)S(1)} %fusion.4), channel_id=1, source_target_pairs={{0,8},{8,0},{16,24},{24,16},{1,9},{9,1},{17,25},{25,17},{2,10},{10... | collective-permute-start | bytes 3145736 | tf_op jit(solution)/shard_map/ppermute | solution.py:192
  697.8 29.5 %collective-permute-start.81 = (bf16[512,1024]{1,0:T(8,128)(2,1)S(1)}, bf16[512,1024]{1,0:T(8,128)(2,1)S(1)}, u32[]{:S(2)}, u32[]{:S(2)}) collective-permute-start(bf16[512,1024]{1,0:T(8,128)(2,1)S(1)} %reduce-precision_convert_fusion.18), channel_id=1, source_target_pairs={{8,16},{16,8},{9,17},{17,9},{10,18},{18,10},{11,19},{19,11},{12,20... | collective-permute-start | bytes 3145736 | tf_op jit(solution)/shard_map/ppermute | solution.py:203
  701.2 24.6 %collective-permute-start.77 = (bf16[512,1024]{1,0:T(8,128)(2,1)S(1)}, bf16[512,1024]{1,0:T(8,128)(2,1)S(1)}, u32[]{:S(2)}, u32[]{:S(2)}) collective-permute-start(bf16[512,1024]{1,0:T(8,128)(2,1)S(1)} %get-tuple-element.1621), channel_id=1, source_target_pairs={{0,4},{2,6},{4,0},{6,2},{1,5},{3,7},{5,1},{7,3},{8,12},{10,14},{12... | collective-permute-start | bytes 3145736 | tf_op jit(solution)/shard_map/ppermute | solution.py:61
  705.6 41.9 %collective-permute-start.85 = (bf16[256,2816]{1,0:T(8,128)(2,1)}, bf16[256,2816]{1,0:T(8,128)(2,1)}, u32[]{:S(2)}, u32[]{:S(2)}) collective-permute-start(bf16[256,2816]{1,0:T(8,128)(2,1)} %broadcast_select_fusion), channel_id=1, source_target_pairs={{0,2},{2,0},{4,6},{6,4},{1,3},{3,1},{5,7},{7,5},{8,10},{10,8},{12,... | collective-permute-start | bytes 4325384 | tf_op jit(solution)/shard_map/ppermute | solution.py:57
  730.3 31.4 %collective-permute-start.83 = (bf16[512,1024]{1,0:T(8,128)(2,1)}, bf16[512,1024]{1,0:T(8,128)(2,1)}, u32[]{:S(2)}, u32[]{:S(2)}) collective-permute-start(bf16[512,1024]{1,0:T(8,128)(2,1)} %fusion.5), channel_id=1, source_target_pairs={{0,8},{8,0},{16,24},{24,16},{1,9},{9,1},{17,25},{25,17},{2,10},{10... | collective-permute-start | bytes 3145736 | tf_op jit(solution)/shard_map/ppermute | solution.py:192
  733.2 28.4 %collective-permute-start.84 = (bf16[512,1024]{1,0:T(8,128)(2,1)}, bf16[512,1024]{1,0:T(8,128)(2,1)}, u32[]{:S(2)}, u32[]{:S(2)}) collective-permute-start(bf16[512,1024]{1,0:T(8,128)(2,1)} %reduce-precision_convert_fusion.16), channel_id=1, source_target_pairs={{8,16},{16,8},{9,17},{17,9},{10,18},{18,10},{11,19},{19,11},{12,20... | collective-permute-start | bytes 3145736 | tf_op jit(solution)/shard_map/ppermute | solution.py:203
  742.5 37.1 %collective-permute-start.79 = (bf16[256,1024]{1,0:T(8,128)(2,1)}, bf16[256,1024]{1,0:T(8,128)(2,1)}, u32[]{:S(2)}, u32[]{:S(2)}) collective-permute-start(bf16[256,1024]{1,0:T(8,128)(2,1)} %get-tuple-element.1641), channel_id=1, source_target_pairs={{0,1},{1,0},{2,3},{3,2},{4,5},{5,4},{6,7},{7,6},{8,9},{9,8},{10,11... | collective-permute-start | bytes 1572872 | tf_op jit(solution)/shard_map/ppermute | solution.py:62
  767.2 33.2 %collective-permute-start.86 = (bf16[512,1024]{1,0:T(8,128)(2,1)}, bf16[512,1024]{1,0:T(8,128)(2,1)}, u32[]{:S(2)}, u32[]{:S(2)}) collective-permute-start(bf16[512,1024]{1,0:T(8,128)(2,1)} %reduce-precision_convert_fusion.13), channel_id=1, source_target_pairs={{8,0},{16,24},{9,1},{17,25},{10,2},{18,26},{11,3},{19,27},{12,4},{... | collective-permute-start | bytes 3145736 | tf_op jit(solution)/shard_map/ppermute | solution.py:200
  768.8 31.7 %collective-permute-start.87 = (bf16[512,1024]{1,0:T(8,128)(2,1)}, bf16[512,1024]{1,0:T(8,128)(2,1)}, u32[]{:S(2)}, u32[]{:S(2)}) collective-permute-start(bf16[512,1024]{1,0:T(8,128)(2,1)} %reduce-precision_convert_fusion.14), channel_id=1, source_target_pairs={{8,16},{16,8},{9,17},{17,9},{10,18},{18,10},{11,19},{19,11},{12,20... | collective-permute-start | bytes 3145736 | tf_op jit(solution)/shard_map/ppermute | solution.py:203
  802.4 28.9 %collective-permute-start.89 = (bf16[512,1024]{1,0:T(8,128)(2,1)S(1)}, bf16[512,1024]{1,0:T(8,128)(2,1)S(1)}, u32[]{:S(2)}, u32[]{:S(2)}) collective-permute-start(bf16[512,1024]{1,0:T(8,128)(2,1)S(1)} %reduce-precision_convert_fusion.12), channel_id=1, source_target_pairs={{8,0},{16,24},{9,1},{17,25},{10,2},{18,26},{11,3},{19,27},{12,4},{... | collective-permute-start | bytes 3145736 | tf_op jit(solution)/shard_map/ppermute | solution.py:200
  (187 other events, 1151.9 us)
